TPU v7x, 32 devices: a whole 2x2x4 slice. The times are simulated.
32 devices in a mesh: entries: 16 (over z, x, core), feat: 2 (over y).
Axes of the slice: x: 2, y: 2, z: 4, core: 2. Of those that a mesh axis runs over, the one named last changes fastest.
Arguments:
- pieces: bfloat16 [4672, 7, 512], P(('entries', 'feat')), may hold values from -6 to 6
- lengths: int32 [4672], P(('entries', 'feat')), may hold values from 1 to 7
- entry_group: int32 [4672], P(('entries', 'feat')), may hold values from 0 to 3
- group_table: bfloat16 [4, 512], P(None, ('entries', 'feat')), may hold values from -6 to 6
- ln1_gain: bfloat16 [512], P(('entries', 'feat')), may hold values from 0.099609375 to 1.8984375
- w_qkv: bfloat16 [512, 1536], P(('entries', 'feat')), may hold values from -0.25 to 0.25
- w_out: bfloat16 [512, 512], P(('entries', 'feat')), may hold values from -0.5 to 0.5
- ln2_gain: bfloat16 [512], P(('entries', 'feat')), may hold values from 0.099609375 to 1.8984375
- w_up: bfloat16 [512, 2048], P(('entries', 'feat')), may hold values from -0.25 to 0.25
- w_down: bfloat16 [2048, 512], P(('entries', 'feat')), may hold values from -0.1875 to 0.1875
- w_proj: bfloat16 [512, 2048], P(('entries', 'feat')), may hold values from -0.25 to 0.25
- text_ids: int32 [9344], replicated, may hold values from 0 to 4671, as said below
- text_mask: int32 [9344], replicated, may hold values from 0 to 1
- grad_embed: bfloat16 [2048, 9344], P(('entries', 'feat')), may hold values from -6 to 6
Outputs:
- embeddings: bfloat16 [2048, 9344], P(('entries', 'feat'))
- grad_pieces: bfloat16 [4672, 7, 512], P(('entries', 'feat'))
- grad_group_table: float32 [4, 512], P(None, ('entries', 'feat'))
- grad_ln1_gain: float32 [512], P(('entries', 'feat'))
- grad_w_qkv: float32 [512, 1536], P(('entries', 'feat'))
- grad_w_out: float32 [512, 512], P(('entries', 'feat'))
- grad_ln2_gain: float32 [512], P(('entries', 'feat'))
- grad_w_up: float32 [512, 2048], P(('entries', 'feat'))
- grad_w_down: float32 [2048, 512], P(('entries', 'feat'))
- grad_w_proj: float32 [512, 2048], P(('entries', 'feat'))
Inputs may be any that keep to these rules, and one draw needn't show every extreme that they name: `text_ids`: every entry is read by at least one text row whose text_mask is 1.
All inputs are finite; a program needn't handle non-finite values.
Results may differ from a plain program's by a relative error of at most 0.012.
Values may be sent and summed in bfloat16 or wider, within the bound.
A program may use at most 128 MiB of HBM per device.

v0:
```python
import functools
import types

import jax
import jax.numpy as jnp
from jax import lax
from jax.experimental import pallas as pl
from jax.experimental.pallas import tpu as pltpu
from jax.sharding import PartitionSpec as P

HEADS = 8
HEAD = 64
PIECES = 7
LANES = 128
TBLOCK = 512
AXES = ("entries", "feat")
MESH = pl.DeviceIdType.MESH
VMEM = pltpu.VMEM
BF16 = jnp.bfloat16
F32 = jnp.float32

epsilon = 1e-05


def contract(left_side, right_side, left_dim, right_dim):
    return lax.dot_general(
        left_side,
        right_side,
        (((left_dim,), (right_dim,)), ((), ())),
        preferred_element_type=jnp.float32,
    )


class Place:
    def __init__(self, n_entries):
        entry = lax.axis_index("entries")
        self.n_z = n_entries // 4
        self.n = n_entries * 2
        self.y = lax.axis_index("feat")
        self.c = lax.rem(entry, 2)
        self.x = lax.rem(lax.div(entry, 2), 2)
        self.z = lax.div(entry, 4)
        self.line = entry * 2 + self.y
        first = self.c == 0
        self.x1 = jnp.where(first, 1 - self.x, self.x)
        self.y1 = jnp.where(first, self.y, 1 - self.y)
        self.x2 = jnp.where(first, self.x, 1 - self.x)
        self.y2 = jnp.where(first, 1 - self.y, self.y)

    def at(self, z, x, c, y):
        return ((z * 2 + x) * 2 + c, y)

    def along_z(self, step):
        return lax.rem(self.z + step, self.n_z)


def meet(place):
    barrier = pltpu.get_barrier_semaphore()

    def greet(step, carry):
        other = lax.rem(place.line + step, place.n)
        pl.semaphore_signal(
            barrier,
            inc=1,
            device_id=(lax.div(other, 2), lax.rem(other, 2)),
            device_id_type=MESH,
        )
        return carry

    lax.fori_loop(1, place.n, greet, 0)
    pl.semaphore_wait(barrier, place.n - 1)


def remote(src, dst, send, recv, to):
    return pltpu.make_async_remote_copy(
        src_ref=src, dst_ref=dst, send_sem=send, recv_sem=recv, device_id=to, device_id_type=MESH
    )


class Gather:
    def __init__(self, place, whole, send, recv):
        p = self.place = place
        nz = p.n_z
        self.nz = nz
        mine = whole.at[p.z, p.x, p.c, p.y]
        self.along = [
            remote(mine, mine, send.at[k - 1], recv.at[k - 1], p.at(p.along_z(k), p.x, p.c, p.y))
            for k in range(1, nz)
        ]
        col = [
            whole.at[:, p.x, p.c, p.y],
            whole.at[:, p.x1, p.c, p.y1],
            whole.at[:, p.x2, p.c, p.y2],
            whole.at[:, 1 - p.x, p.c, 1 - p.y],
        ]
        to_one = p.at(p.z, p.x1, p.c, p.y1)
        to_two = p.at(p.z, p.x2, p.c, p.y2)
        to_core = p.at(p.z, p.x, 1 - p.c, p.y)
        s = nz - 1
        self.one = remote(col[0], col[0], send.at[s], recv.at[s], to_one)
        self.two = remote(col[0], col[0], send.at[s + 1], recv.at[s + 1], to_two)
        self.three = remote(col[1], col[1], send.at[s + 2], recv.at[s + 2], to_two)
        self.core = [
            remote(col[k], col[k], send.at[s + 3 + k], recv.at[s + 3 + k], to_core)
            for k in range(4)
        ]

    def step(self, stage):
        if stage == 0:
            for copy in self.along:
                copy.start()
        elif stage == 1:
            for copy in self.along:
                copy.wait_recv()
            self.one.start()
            self.two.start()
            self.core[0].start()
        elif stage == 2:
            self.one.wait_recv()
            self.three.start()
            self.core[1].start()
        elif stage == 3:
            self.two.wait_recv()
            self.core[2].start()
        elif stage == 4:
            self.three.wait_recv()
            self.core[3].start()
        elif stage == 5:
            for copy in self.core:
                copy.wait_recv()

    def finish(self):
        for copy in self.along + [self.one, self.two, self.three] + self.core:
            copy.wait_send()


class Reduce:
    def __init__(self, place, parts, held_core, held_one, held_two, held_z, send, recv):
        p = self.place = place
        nz = p.n_z
        self.parts, self.held_core = parts, held_core
        self.held_one, self.held_two, self.held_z = held_one, held_two, held_z
        self.cols = [(p.x, p.y), (p.x1, p.y1), (p.x2, p.y2), (1 - p.x, 1 - p.y)]
        to_one = p.at(p.z, p.x1, p.c, p.y1)
        to_two = p.at(p.z, p.x2, p.c, p.y2)
        to_core = p.at(p.z, p.x, 1 - p.c, p.y)

        def col(k):
            return parts.at[:, self.cols[k][0], p.c, self.cols[k][1]]

        self.core = remote(parts.at[:, :, 1 - p.c], held_core, send.at[0], recv.at[0], to_core)
        self.one = [
            remote(col(1), held_one.at[0], send.at[1], recv.at[1], to_one),
            remote(col(3), held_one.at[1], send.at[2], recv.at[2], to_one),
        ]
        self.two = remote(col(2), held_two, send.at[3], recv.at[3], to_two)
        self.along = [
            remote(
                parts.at[p.along_z(k), p.x, p.c, p.y],
                held_z.at[k - 1],
                send.at[3 + k],
                recv.at[3 + k],
                p.at(p.along_z(k), p.x, p.c, p.y),
            )
            for k in range(1, nz)
        ]

    def add(self, k, other):
        p, (x, y) = self.place, self.cols[k]
        self.parts[:, x, p.c, y] = (
            self.parts[:, x, p.c, y].astype(F32) + other.astype(F32)
        ).astype(BF16)

    def step(self, stage, out=None):
        if stage == 0:
            self.core.start()
        elif stage == 1:
            self.core.wait_recv()
            for k in (3, 1, 2, 0):
                x, y = self.cols[k]
                self.add(k, self.held_core[:, x, y])
                if k == 3:
                    self.one[1].start()
                if k == 1:
                    self.one[0].start()
        elif stage == 2:
            self.one[1].wait_recv()
            self.add(2, self.held_one[1])
            self.two.start()
            self.one[0].wait_recv()
            self.add(0, self.held_one[0])
        elif stage == 3:
            self.two.wait_recv()
            self.add(0, self.held_two[...])
            for copy in self.along:
                copy.start()
        elif stage == 4:
            p = self.place
            total = self.parts[p.z, p.x, p.c, p.y].astype(F32)
            for k, copy in enumerate(self.along):
                copy.wait_recv()
                total = total + self.held_z[k].astype(F32)
            out[...] = total

    def finish(self):
        for copy in [self.core] + self.one + [self.two] + self.along:
            copy.wait_send()


def exchange(place, src, dst, send, recv):
    dst[place.line] = src[place.line]

    def begin(step, carry):
        other = lax.rem(place.line + step, place.n)
        remote(
            src.at[other],
            dst.at[place.line],
            send.at[step],
            recv.at[step],
            (lax.div(other, 2), lax.rem(other, 2)),
        ).start()
        return carry

    lax.fori_loop(1, place.n, begin, 0)


def exchange_wait(place, src, dst, send, recv, sends):
    def end(step, carry):
        other = lax.rem(place.line + step, place.n)
        copy = remote(
            src.at[other],
            dst.at[place.line],
            send.at[step],
            recv.at[step],
            (lax.div(other, 2), lax.rem(other, 2)),
        )
        if sends:
            copy.wait_send()
        else:
            copy.wait_recv()
        return carry

    lax.fori_loop(1, place.n, end, 0)


def text_blocks(length):
    whole = length // TBLOCK
    return whole, length - whole * TBLOCK


def one_hot(keys, depth):
    width = keys.shape[1]
    return (lax.broadcasted_iota(jnp.int32, (depth, width), 0) == keys).astype(F32).astype(BF16)


def scatter_block(start, width, row_ref, seg_ref, cot_ref, acc_ref):
    span = pl.ds(start, width)
    hot = one_hot(row_ref[:, span], acc_ref.shape[0])
    seg = seg_ref[:, span]
    cot = cot_ref[:, span].astype(F32)
    segments = acc_ref.shape[1] // cot.shape[0]
    spread = jnp.concatenate(
        [jnp.where(seg == q, cot, 0.0).astype(BF16) for q in range(segments)], axis=0
    )
    acc_ref[...] += contract(hot, spread, 1, 1)


def lookup_block(start, width, row_ref, seg_ref, table_ref, out_ref):
    span = pl.ds(start, width)
    hot = one_hot(row_ref[:, span], table_ref.shape[1])
    seg = seg_ref[:, span]
    wide = jnp.dot(table_ref[...], hot, preferred_element_type=F32)
    feats = out_ref.shape[0]
    found = jnp.zeros((feats, width), F32)
    for q in range(table_ref.shape[0] // feats):
        found = found + jnp.where(seg == q, wide[q * feats : (q + 1) * feats], 0.0)
    out_ref[:, span] = found.astype(BF16)


N_WEIGHTS = 5


def gather_kernel(n_entries, *refs):
    shards = refs[:N_WEIGHTS]
    row_ref, seg_ref, cot_ref = refs[N_WEIGHTS : N_WEIGHTS + 3]
    wholes = refs[N_WEIGHTS + 3 : 2 * N_WEIGHTS + 3]
    back_ref = refs[2 * N_WEIGHTS + 3]
    acc_ref, sent_ref, g_send, g_recv, x_send, x_recv = refs[2 * N_WEIGHTS + 4 :]
    place = Place(n_entries)
    n = place.n
    gathers = [
        Gather(place, whole, g_send.at[i], g_recv.at[i]) for i, whole in enumerate(wholes)
    ]
    for shard, whole in zip(shards, wholes):
        whole[place.z, place.x, place.c, place.y] = shard[...]
    acc_ref[...] = jnp.zeros_like(acc_ref)
    meet(place)
    slots = N_WEIGHTS + 5
    whole_blocks, tail = text_blocks(row_ref.shape[1])
    for slot in range(slots):
        for i in range(N_WEIGHTS):
            if 0 <= slot - i <= 5:
                gathers[i].step(slot - i)
        low, high = slot * whole_blocks // slots, (slot + 1) * whole_blocks // slots

        def block(i, carry):
            scatter_block(
                pl.multiple_of(i * TBLOCK, TBLOCK), TBLOCK, row_ref, seg_ref, cot_ref, acc_ref
            )
            return carry

        lax.fori_loop(low, high, block, 0)
    if tail:
        scatter_block(whole_blocks * TBLOCK, tail, row_ref, seg_ref, cot_ref, acc_ref)
    half, rows = n // 2, sent_ref.shape[1]

    def pack(i, carry):
        span = pl.ds(pl.multiple_of(i * rows, rows), rows)
        sent_ref[i] = acc_ref[span, :LANES].astype(BF16)
        sent_ref[i + half] = acc_ref[span, LANES:].astype(BF16)
        return carry

    lax.fori_loop(0, half, pack, 0)
    exchange(place, sent_ref, back_ref, x_send, x_recv)
    exchange_wait(place, sent_ref, back_ref, x_send, x_recv, False)
    exchange_wait(place, sent_ref, back_ref, x_send, x_recv, True)
    for gather in gathers:
        gather.finish()


def reduce_kernel(n_entries, *refs):
    grads = refs[:N_WEIGHTS]
    sent_ref, row_ref, seg_ref = refs[N_WEIGHTS : N_WEIGHTS + 3]
    outs = refs[N_WEIGHTS + 3 : 2 * N_WEIGHTS + 3]
    found_ref = refs[2 * N_WEIGHTS + 3]
    scratch = refs[2 * N_WEIGHTS + 4 :]
    held = scratch[: 4 * N_WEIGHTS]
    came_ref, table_ref, r_send, r_recv, x_send, x_recv = scratch[4 * N_WEIGHTS :]
    place = Place(n_entries)
    n = place.n
    reduces = [
        Reduce(place, grads[i], *held[4 * i : 4 * i + 4], r_send.at[i], r_recv.at[i])
        for i in range(N_WEIGHTS)
    ]
    meet(place)
    for reduce in reduces:
        reduce.step(0)
    exchange(place, sent_ref, came_ref, x_send, x_recv)
    order = (4, 3, 2, 1, 0)
    for i in order:
        reduces[i].step(1)
    exchange_wait(place, sent_ref, came_ref, x_send, x_recv, False)
    half, rows = n // 2, sent_ref.shape[1]
    for side in range(2):
        part = came_ref[side * half : (side + 1) * half].reshape(half * rows, LANES)
        table_ref[side * LANES : (side + 1) * LANES, :] = part.astype(F32).T.astype(BF16)
    slots = N_WEIGHTS + 2
    whole_blocks, tail = text_blocks(row_ref.shape[1])
    for slot in range(slots):
        for k, i in enumerate(order):
            if 2 <= slot - k + 2 <= 4:
                reduces[i].step(slot - k + 2, outs[i])
        low, high = slot * whole_blocks // slots, (slot + 1) * whole_blocks // slots

        def block(i, carry):
            lookup_block(
                pl.multiple_of(i * TBLOCK, TBLOCK), TBLOCK, row_ref, seg_ref, table_ref, found_ref
            )
            return carry

        lax.fori_loop(low, high, block, 0)
    if tail:
        lookup_block(whole_blocks * TBLOCK, tail, row_ref, seg_ref, table_ref, found_ref)
    exchange_wait(place, sent_ref, came_ref, x_send, x_recv, True)
    for reduce in reduces:
        reduce.finish()


def cast_pair(value):
    high = value.astype(BF16)
    return high, (value - high.astype(F32)).astype(BF16)


def head_ones():
    head_row = lax.broadcasted_iota(jnp.int32, (4 * HEAD, 4 * HEAD), 0) // HEAD
    head_col = lax.broadcasted_iota(jnp.int32, (4 * HEAD, 4 * HEAD), 1) // HEAD
    return (head_row == head_col).astype(F32).astype(BF16)


def head_sum(value, ones):
    high, low = cast_pair(value)
    step = 4 * HEAD
    return jnp.concatenate(
        [
            jnp.dot(high[:, j : j + step], ones, preferred_element_type=F32)
            + jnp.dot(low[:, j : j + step], ones, preferred_element_type=F32)
            for j in range(0, value.shape[1], step)
        ],
        axis=1,
    )


def flat(ref, low=None, high=None):
    value = ref[...] if low is None else ref[:, :, :, :, :, low:high]
    return value.reshape(-1, value.shape[-1])


def spread_segments(blocks, feats, segs):
    lane = lax.broadcasted_iota(jnp.int32, blocks[0].shape, 1) // feats
    out = []
    for h in range(segs):
        whole = None
        for j in range(segs):
            shift = ((j - h) * feats) % LANES
            moved = blocks[j] if shift == 0 else pltpu.roll(blocks[j], shift, 1)
            whole = moved if whole is None else jnp.where(lane == j, moved, whole)
        out.append(whole)
    return out


class Block:
    def __init__(self, m, segs, seg_rows, rows, feats):
        self.m, self.segs, self.seg_rows, self.rows, self.feats = m, segs, seg_rows, rows, feats
        self.number = m.pieces.shape[0]
        self.width = m.pieces.shape[2]
        self.total = segs * rows

    def pieces_of(self, h):
        return min(self.seg_rows, max(self.number - h * self.seg_rows, 0))

    def load(self):
        m = self.m
        for k in range(self.width // LANES):
            lanes = slice(k * LANES, (k + 1) * LANES)
            m.layout[k, 0 : self.number, 0:PIECES, :] = m.pieces[:, :, lanes].astype(F32)
            lines = m.layout.at[k].reshape(self.total * 8, LANES)
            for h in range(self.segs):
                count = self.pieces_of(h)
                base = h * self.rows
                for p in range(PIECES):
                    m.unit[p, base : base + count, lanes] = lines[
                        pl.ds(h * self.seg_rows * 8 + p, count, stride=8), :
                    ]
                    if count < self.rows:
                        m.unit[p, base + count : base + self.rows, lanes] = jnp.zeros(
                            (self.rows - count, LANES), F32
                        )

    def norm_one(self):
        m, width = self.m, self.width
        small = flat(m.w_qkv, 3 * width, 3 * width + LANES).astype(F32).T
        m.small[...] = small[:8]
        start = m.unit[0]
        for g in range(m.n_groups):
            start = start + jnp.where(m.groups[...] == g, small[2 + g : 3 + g, :], 0.0)
        m.unit[0] = start
        m.first[...] = start

        def one(p, carry):
            value = m.unit[p]
            centered = value - jnp.mean(value, axis=1, keepdims=True)
            inv = lax.rsqrt(jnp.mean(centered * centered, axis=1, keepdims=True) + epsilon)
            unit = centered * inv
            m.unit[p] = unit
            m.inv_one[p] = jnp.broadcast_to(inv, (self.total, LANES))
            m.normed[p] = (unit * m.small[0:1, :]).astype(BF16)
            return carry

        lax.fori_loop(0, PIECES, one, 0)

    def project_qkv(self):
        m, width = self.m, self.width
        step = 2 * LANES
        m.query[...] = jnp.dot(
            m.normed[0], flat(m.w_qkv, 0, width), preferred_element_type=F32
        ).astype(BF16)

        def one(j, carry):
            span = pl.ds(pl.multiple_of(j * step, step), step)
            source = pl.ds(pl.multiple_of(width + j * step, step), step)
            weight = m.w_qkv[:, :, :, :, :, source].reshape(width, step)
            m.key_value[:, :, span] = (
                jnp.dot(
                    m.normed[...].reshape(PIECES * self.total, width),
                    weight,
                    preferred_element_type=F32,
                )
                .astype(BF16)
                .reshape(PIECES, self.total, step)
            )
            return carry

        lax.fori_loop(0, 2 * width // step, one, 0)

    def attend(self):
        m, width = self.m, self.width
        ones = head_ones()

        def score(p, carry):
            product = m.query[...].astype(F32) * m.key_value[p, :, :width].astype(F32)
            m.prob[p] = head_sum(product, ones) * (HEAD**-0.5)
            return carry

        lax.fori_loop(0, PIECES, score, 0)

        def soft(i, carry):
            span = pl.ds(pl.multiple_of(i * 16, 16), 16)
            length = m.lengths[span, :]
            scores = [
                jnp.where(p < length, m.prob[p, span, :], -1e30) for p in range(PIECES)
            ]
            highest = functools.reduce(jnp.maximum, scores)
            raised = [jnp.exp(s - highest) for s in scores]
            inv = 1.0 / functools.reduce(jnp.add, raised)
            total = jnp.zeros((16, width), F32)
            for p in range(PIECES):
                prob = raised[p] * inv
                m.prob[p, span, :] = prob
                total = total + prob.astype(BF16).astype(F32) * m.key_value[
                    p, span, width:
                ].astype(F32)
            m.attended[span, :] = total.astype(BF16)
            return carry

        lax.fori_loop(0, self.total // 16, soft, 0)

    def norm_two(self):
        m, width = self.m, self.width
        hidden = m.first[...] + jnp.dot(
            m.attended[...], flat(m.w_out), preferred_element_type=F32
        )
        m.hidden[...] = hidden
        centered = hidden - jnp.mean(hidden, axis=1, keepdims=True)
        inv = lax.rsqrt(jnp.mean(centered * centered, axis=1, keepdims=True) + epsilon)
        unit = centered * inv
        m.unit_two[...] = unit
        m.inv_two[...] = jnp.broadcast_to(inv, (self.total, LANES))
        m.normed_two[...] = (unit * m.small[1:2, :]).astype(BF16)

    def up(self):
        m, step = self.m, 2 * LANES

        def one(j, carry):
            span = pl.ds(pl.multiple_of(j * step, step), step)
            weight = m.w_up[:, :, :, :, :, span].reshape(self.width, step)
            upward = jnp.dot(m.normed_two[...], weight, preferred_element_type=F32)
            normal = 0.5 * (1.0 + lax.erf(upward * (0.5**0.5)))
            m.activated[:, span] = (upward * normal).astype(BF16)
            m.slope[:, span] = normal + upward * (
                jnp.exp(-0.5 * upward * upward) * 0.3989422804014327
            )
            return carry

        lax.fori_loop(0, m.activated.shape[1] // step, one, 0)

    def down(self):
        m = self.m
        m.output[...] = (
            m.hidden[...]
            + jnp.dot(m.activated[...], flat(m.w_down), preferred_element_type=F32)
        ).astype(BF16)

    def table(self):
        m, segs, rows = self.m, self.segs, self.rows

        def one(g, carry):
            span = pl.ds(pl.multiple_of(g * LANES, LANES), LANES)
            weight = m.w_proj[:, :, :, :, :, span].reshape(self.width, LANES)
            value = jnp.dot(m.output[...], weight, preferred_element_type=F32)
            parts = [value[h * rows : (h + 1) * rows] for h in range(segs)]
            for j, part in enumerate(spread_segments(parts, self.feats, segs)):
                m.sent[g * segs + j] = part.astype(BF16)
            return carry

        lax.fori_loop(0, m.w_proj.shape[-1] // LANES, one, 0)


    def table_back(self):
        m, segs, rows = self.m, self.segs, self.rows

        def one(g, carry):
            span = pl.ds(pl.multiple_of(g * LANES, LANES), LANES)
            parts = [m.came[g * segs + j].astype(F32) for j in range(segs)]
            for h, part in enumerate(spread_segments(parts, self.feats, segs)):
                m.grad_table[h * rows : (h + 1) * rows, span] = part.astype(BF16)
            return carry

        lax.fori_loop(0, m.grad_table.shape[1] // LANES, one, 0)

    def put(self, ref, value):
        ref[...] = value.astype(BF16).reshape(ref.shape)

    def proj_back(self):
        m = self.m
        self.put(m.d_proj, contract(m.output[...], m.grad_table[...], 0, 0))
        grad_output = contract(m.grad_table[...], flat(m.w_proj), 1, 1)
        m.grad_output[...] = grad_output
        m.grad_branch[...] = grad_output.astype(BF16)

    def down_back(self):
        m = self.m
        self.put(m.d_down, contract(m.activated[...], m.grad_branch[...], 0, 0))
        grad_act = contract(m.grad_branch[...], flat(m.w_down), 1, 1)
        m.grad_up[...] = (grad_act * m.slope[...]).astype(BF16)

    def up_back(self):
        m = self.m
        self.put(m.d_up, contract(m.normed_two[...], m.grad_up[...], 0, 0))
        grad = contract(m.grad_up[...], flat(m.w_up), 1, 1)
        m.d_small[...] = jnp.zeros_like(m.d_small)
        unit = m.unit_two[...]
        m.d_small[1:2, :] = jnp.sum(grad * unit, axis=0, keepdims=True)
        grad = grad * m.small[1:2, :]
        first = jnp.mean(grad, axis=1, keepdims=True)
        second = jnp.mean(grad * unit, axis=1, keepdims=True)
        hidden = m.grad_output[...] + m.inv_two[:, 0:1] * (grad - first - unit * second)
        m.hidden[...] = hidden
        m.grad_branch[...] = hidden.astype(BF16)

    def out_back(self):
        m = self.m
        self.put(m.d_out, contract(m.attended[...], m.grad_branch[...], 0, 0))
        m.grad_att[...] = contract(m.grad_branch[...], flat(m.w_out), 1, 1).astype(BF16)

    def attend_back(self):
        m, width = self.m, self.width
        ones = head_ones()
        scale = HEAD**-0.5

        def score(p, carry):
            product = m.grad_att[...].astype(F32) * m.key_value[p, :, width:].astype(F32)
            m.grad_prob[p] = head_sum(product, ones)
            return carry

        lax.fori_loop(0, PIECES, score, 0)

        def soft(i, carry):
            span = pl.ds(pl.multiple_of(i * 16, 16), 16)
            inner = jnp.zeros((16, width), F32)
            for p in range(PIECES):
                inner = inner + m.prob[p, span, :] * m.grad_prob[p, span, :]
            query = m.query[span, :].astype(F32)
            grad_att = m.grad_att[span, :].astype(F32)
            grad_query = jnp.zeros((16, width), F32)
            for p in range(PIECES):
                prob = m.prob[p, span, :]
                low = prob.astype(BF16).astype(F32)
                grad = (prob * (m.grad_prob[p, span, :] - inner)).astype(BF16).astype(F32)
                grad_query = grad_query + grad * m.key_value[p, span, :width].astype(F32)
                m.grad_kv[p, span, :width] = (grad * query * scale).astype(BF16)
                m.grad_kv[p, span, width:] = (low * grad_att).astype(BF16)
            m.grad_query[span, :] = (grad_query * scale).astype(BF16)
            return carry

        lax.fori_loop(0, self.total // 16, soft, 0)

    def qkv_back(self):
        m, width = self.m, self.width
        lead = m.d_qkv.shape[:-1]
        step = 2 * LANES
        m.d_qkv[:, :, :, :, :, :width] = (
            contract(m.normed[0], m.grad_query[...], 0, 0).astype(BF16).reshape(lead + (width,))
        )

        def one(j, carry):
            target = pl.ds(pl.multiple_of(width + j * step, step), step)
            span = pl.ds(pl.multiple_of(j * step, step), step)
            grad = m.grad_kv[:, :, span].reshape(PIECES * self.total, step)
            m.d_qkv[:, :, :, :, :, target] = (
                contract(m.normed[...].reshape(PIECES * self.total, width), grad, 0, 0)
                .astype(BF16)
                .reshape(lead + (step,))
            )
            return carry

        lax.fori_loop(0, 2 * width // step, one, 0)

    def normed_back(self):
        m, width = self.m, self.width
        m.grad_prob[...] = contract(
            m.grad_kv[...].reshape(PIECES * self.total, 2 * width),
            flat(m.w_qkv, width, 3 * width),
            1,
            1,
        ).reshape(PIECES, self.total, width)
        m.grad_prob[0] += contract(m.grad_query[...], flat(m.w_qkv, 0, width), 1, 1)

    def norm_back(self):
        m, width = self.m, self.width
        gain = m.small[0:1, :]

        def back(p):
            grad = m.grad_prob[p]
            unit = m.unit[p]
            m.d_small[0:1, :] += jnp.sum(grad * unit, axis=0, keepdims=True)
            grad = grad * gain
            first = jnp.mean(grad, axis=1, keepdims=True)
            second = jnp.mean(grad * unit, axis=1, keepdims=True)
            grad = m.inv_one[p][:, 0:1] * (grad - first - unit * second)
            if p == 0:
                grad = grad + m.hidden[...]
                for g in range(m.n_groups):
                    m.d_small[2 + g : 3 + g, :] = jnp.sum(
                        jnp.where(m.groups[...] == g, grad, 0.0), axis=0, keepdims=True
                    )
            for k in range(width // LANES):
                lines = m.layout.at[k].reshape(self.total * 8, LANES)
                for h in range(self.segs):
                    count = self.pieces_of(h)
                    lines[pl.ds(h * self.seg_rows * 8 + p, count, stride=8), :] = grad[
                        h * self.rows : h * self.rows + count, k * LANES : (k + 1) * LANES
                    ]

        for p in range(PIECES):
            back(p)
        for k in range(width // LANES):
            m.grad_pieces[:, :, k * LANES : (k + 1) * LANES] = m.layout[
                k, 0 : self.number, 0:PIECES, :
            ].astype(BF16)
        lead = m.d_qkv.shape[:-1]
        small = jnp.concatenate(
            [m.d_small[...], jnp.zeros((LANES - 8, width), F32)], axis=0
        ).T
        m.d_qkv[:, :, :, :, :, 3 * width :] = small.astype(BF16).reshape(lead + (LANES,))


def block_scratch(n, rows, total, width, hidden, out_width):
    return dict(
        layout=((width // LANES, total, 8, LANES), F32),
        unit=((PIECES, total, width), F32),
        inv_one=((PIECES, total, LANES), F32),
        first=((total, width), F32),
        small=((8, width), F32),
        normed=((PIECES, total, width), BF16),
        query=((total, width), BF16),
        key_value=((PIECES, total, 2 * width), BF16),
        prob=((PIECES, total, width), F32),
        attended=((total, width), BF16),
        hidden=((total, width), F32),
        unit_two=((total, width), F32),
        inv_two=((total, LANES), F32),
        normed_two=((total, width), BF16),
        activated=((total, hidden), BF16),
        slope=((total, hidden), F32),
        output=((total, width), BF16),
        grad_table=((total, out_width), BF16),
        grad_output=((total, width), F32),
        grad_branch=((total, width), BF16),
        grad_up=((total, hidden), BF16),
        d_small=((8, width), F32),
        grad_att=((total, width), BF16),
        grad_prob=((PIECES, total, width), F32),
        grad_kv=((PIECES, total, 2 * width), BF16),
        grad_query=((total, width), BF16),
    )


def middle_kernel(names, consts, *refs):
    m = types.SimpleNamespace(**dict(zip(names, refs)), n_groups=consts[0])
    block = Block(m, *consts[1:])
    block.load()
    block.norm_one()
    block.project_qkv()
    block.attend()
    block.norm_two()
    block.up()
    block.down()
    block.table()
    block.table_back()
    block.proj_back()
    block.down_back()
    block.up_back()
    block.out_back()
    block.attend_back()
    block.qkv_back()
    block.normed_back()
    block.norm_back()


def full(shape, dtype):
    return jax.ShapeDtypeStruct(shape, dtype)


def body(
    mesh_shape,
    pieces,
    lengths,
    entry_group,
    group_table,
    ln1_gain,
    w_qkv,
    w_out,
    ln2_gain,
    w_up,
    w_down,
    w_proj,
    text_ids,
    text_mask,
    grad_embed,
):
    n_entries = mesh_shape["entries"]
    n = n_entries * mesh_shape["feat"]
    n_z = n_entries // 4
    number, width = pieces.shape[0], pieces.shape[2]
    shard = ln1_gain.shape[0]
    groups_n = group_table.shape[0]
    feats = grad_embed.shape[0]
    text_len = text_ids.shape[0]
    segs = LANES // feats
    seg_rows = -(-number // segs)
    rows = -(-seg_rows // 16) * 16
    half = n // 2

    small = jnp.concatenate([ln1_gain[:, None], ln2_gain[:, None], group_table.T], axis=1)
    w_qkv_more = jnp.concatenate(
        [w_qkv, jnp.pad(small, ((0, 0), (0, LANES - small.shape[1])))], axis=1
    )
    total = segs * rows

    def column(values):
        values = jnp.pad(values, (0, segs * seg_rows - number)).reshape(segs, seg_rows)
        return jnp.pad(values, ((0, 0), (0, rows - seg_rows))).reshape(total, 1)

    source = text_ids // number
    within = text_ids - source * number
    segment = within // seg_rows
    row_key = (source % half) * rows + within - segment * seg_rows
    seg_key = jnp.where(text_mask != 0, (source // half) * segs + segment, -1)
    row_key, seg_key = row_key[None, :], seg_key[None, :]

    vmem = pl.BlockSpec(memory_space=VMEM)
    shards = (w_qkv_more, w_out, w_up, w_down, w_proj)
    lead = (n_z, 2, 2, 2)
    gathered = pl.pallas_call(
        functools.partial(gather_kernel, n_entries),
        out_shape=tuple(full(lead + s.shape, BF16) for s in shards)
        + (full((n, rows, LANES), BF16),),
        in_specs=[vmem] * 8,
        out_specs=(vmem,) * 6,
        scratch_shapes=[
            VMEM((half * rows, 2 * LANES), F32),
            VMEM((n, rows, LANES), BF16),
            pltpu.SemaphoreType.DMA((N_WEIGHTS, n_z + 6)),
            pltpu.SemaphoreType.DMA((N_WEIGHTS, n_z + 6)),
            pltpu.SemaphoreType.DMA((n,)),
            pltpu.SemaphoreType.DMA((n,)),
        ],
        compiler_params=pltpu.CompilerParams(
            collective_id=0, has_side_effects=True, vmem_limit_bytes=56 * 2**20
        ),
    )(*shards, row_key, seg_key, grad_embed)
    *wholes, came = gathered
    ins = dict(
        pieces=pieces,
        lengths=column(lengths),
        groups=column(entry_group),
        w_qkv=wholes[0],
        w_out=wholes[1],
        w_up=wholes[2],
        w_down=wholes[3],
        w_proj=wholes[4],
        came=came,
    )
    outs = dict(
        d_qkv=full(lead + w_qkv_more.shape, BF16),
        d_out=full(lead + w_out.shape, BF16),
        d_up=full(lead + w_up.shape, BF16),
        d_down=full(lead + w_down.shape, BF16),
        d_proj=full(lead + w_proj.shape, BF16),
        sent=full((n, rows, LANES), BF16),
        grad_pieces=full(pieces.shape, BF16),
    )
    scratch = block_scratch(n, rows, total, width, w_up.shape[1], w_proj.shape[1])
    *grads, blocks, grad_pieces = pl.pallas_call(
        functools.partial(
            middle_kernel,
            tuple(ins) + tuple(outs) + tuple(scratch),
            (groups_n, segs, seg_rows, rows, feats),
        ),
        out_shape=tuple(outs.values()),
        in_specs=[vmem] * len(ins),
        out_specs=(vmem,) * len(outs),
        scratch_shapes=[VMEM(*item) for item in scratch.values()],
        compiler_params=pltpu.CompilerParams(vmem_limit_bytes=60 * 2**20),
    )(*ins.values())
    held = []
    for s in shards:
        held += [
            VMEM((n_z, 2, 2) + s.shape, BF16),
            VMEM((2, n_z) + s.shape, BF16),
            VMEM((n_z,) + s.shape, BF16),
            VMEM((n_z - 1,) + s.shape, BF16),
        ]
    summed = pl.pallas_call(
        functools.partial(reduce_kernel, n_entries),
        out_shape=tuple(full(s.shape, F32) for s in shards) + (full((feats, text_len), BF16),),
        in_specs=[vmem] * 8,
        out_specs=(vmem,) * 6,
        scratch_shapes=held
        + [
            VMEM((n, rows, LANES), BF16),
            VMEM((2 * LANES, half * rows), BF16),
            pltpu.SemaphoreType.DMA((N_WEIGHTS, n_z + 4)),
            pltpu.SemaphoreType.DMA((N_WEIGHTS, n_z + 4)),
            pltpu.SemaphoreType.DMA((n,)),
            pltpu.SemaphoreType.DMA((n,)),
        ],
        compiler_params=pltpu.CompilerParams(
            collective_id=1, has_side_effects=True, vmem_limit_bytes=56 * 2**20
        ),
    )(*grads, blocks, row_key, seg_key)
    s_qkv, s_out, s_up, s_down, s_proj, embeddings = summed
    s_small = s_qkv[:, 3 * width :]
    return (
        embeddings,
        grad_pieces,
        s_small[:, 2 : 2 + groups_n].T,
        s_small[:, 0],
        s_qkv[:, : 3 * width],
        s_out,
        s_small[:, 1],
        s_up,
        s_down,
        s_proj,
    )


def solution(mesh):
    both = P(AXES)
    rows = P(AXES, None)
    return jax.shard_map(
        functools.partial(body, dict(mesh.shape)),
        mesh=mesh,
        in_specs=(
            P(AXES, None, None),
            both,
            both,
            P(None, AXES),
            both,
            rows,
            rows,
            both,
            rows,
            rows,
            rows,
            P(),
            P(),
            rows,
        ),
        out_specs=(
            rows,
            P(AXES, None, None),
            P(None, AXES),
            both,
            rows,
            rows,
            both,
            rows,
            rows,
            rows,
        ),
        check_vma=False,
    )
```

profile of v0, /device:TPU:0, one launch (start us, length us, event | category | flops | bytes accessed | tf_op | source)
XLA Modules:
  0.0 206.1 jit_solution(17983471122404180088)
XLA Ops:
  0.6 0.8 reshape.32
  1.4 0.8 reshape.34
  2.2 0.8 copy.30
  2.9 0.7 copy.31
  3.7 0.7 copy.32
  4.4 0.1 fusion.14
  4.5 1.4 pad_maximum_fusion.refs_0_
  5.9 0.8 reshape.37.refs_2_
  6.7 0.8 reshape.36.refs_1_
  7.5 0.9 fusion.5
  8.4 0.6 broadcast_in_dim.17.refs_6_.refs_7_
  9.1 0.6 broadcast_in_dim.16.refs_5_.refs_6_
  9.7 2.6 %copy.33.refs_0_ = bf16[146,7,512]{2,1,0:T(8,128)(2,1)} copy(bf16[146,7,512]{2,0,1:T(8,128)(2,1)} %param.14) | data formatting | bytes 2093056 | tf_op args[0]
  12.3 74.4 %shard_map.213 = (bf16[4,2,2,2,16,1664]{5,4,3,2,1,0:T(8,128)(2,1)}, bf16[4,2,2,2,16,512]{5,4,3,2,1,0:T(8,128)(2,1)}, bf16[4,2,2,2,16,2048]{5,4,3,2,1,0:T(8,128)(...) custom-call(bf16[16,1664]{1,0:T(8,128)(2,1)} %pad_maximum_fusion.ref, ...), custom_call_target="tpu_custom_call" | custom-call | tf_op jit(solution)/shard_map/pallas_call | solution.py:834
  86.8 35.3 %shard_map.214 = (bf16[4,2,2,2,16,1664]{5,4,3,2,1,0:T(8,128)(2,1)}, bf16[4,2,2,2,16,512]{5,4,3,2,1,0:T(8,128)(2,1)}, bf16[4,2,2,2,16,2048]{5,4,3,2,1,0:T(8,128)(...) custom-call(bf16[146,7,512]{2,1,0:T(8,128)(2,1)} %copy.33.refs_0_, ...), custom_call_target="tpu_custom_call" | custom-call | tf_op jit(solution)/shard_map/pallas_call | solution.py:874
  122.0 0.0 copy-start
  122.1 74.6 %shard_map.215 = (f32[16,1664]{1,0:T(8,128)}, f32[16,512]{1,0:T(8,128)}, f32[16,2048]{1,0:T(8,128)}, f32[64,512]{1,0:T(8,128)}, f32[16,2048]{1,0:T(8,128)}, /*index=5*/bf16[64,9344]{1,0:T(8,128)(2,1)}) custom-call(bf16[4,2,2,2,16,1664]{5,4,3,2,1,0:T(8,128)(2,1)} %get-tuple-element.35.refs_0_, bf16[4,2,2,2,16,512]{5,4,3,2,1,0:T(8,128)(2,1)} %get-tuple-element.36.refs_1_, ...), custom_call_target="tpu_custom_call" | custom-call | tf_op jit(solution)/shard_map/pallas_call | solution.py:894
  196.6 0.0 copy-start.1
  196.6 1.5 slice_reduce_fusion
  198.1 0.8 slice_bitcast_fusion
  198.9 1.5 slice.18
  200.4 0.7 copy.37
  201.1 0.0 copy-done
  201.1 1.3 copy.36
  202.4 0.0 copy-done.1
  202.4 0.0 copy-start.5
  202.4 0.0 copy-start.4
  202.4 0.0 copy-start.3
  202.4 0.0 copy-start.2
  202.5 1.0 copy.43
  203.5 0.0 copy-done.5
  203.5 0.6 copy.44
  204.1 0.0 copy-done.4
  204.1 0.7 copy.45
  204.8 0.0 copy-done.3
  204.8 0.7 copy.46
  205.4 0.0 copy-done.2
  205.4 0.7 copy.47
  (2 shorter events, 0.0 us)
Async XLA Ops:
  122.0 79.0 %copy-start = (bf16[146,7,512]{2,1,0:T(8,128)(2,1)S(1)}, bf16[146,7,512]{2,1,0:T(8,128)(2,1)}, u32[]{:S(2)}) copy-start(bf16[146,7,512]{2,1,0:T(8,128)(2,1)} %get-tuple-element.59) | copy-start | bytes 3139588
  196.6 5.8 %copy-start.1 = (bf16[64,9344]{1,0:T(8,128)(2,1)S(1)}, bf16[64,9344]{1,0:T(8,128)(2,1)}, u32[]{:S(2)}) copy-start(bf16[64,9344]{1,0:T(8,128)(2,1)} %get-tuple-element.82) | copy-start | bytes 3588100
  202.4 1.0 copy-start.5
  202.4 1.7 copy-start.4
  202.4 2.3 %copy-start.3 = (f32[64,512]{1,0:T(8,128)S(1)}, f32[64,512]{1,0:T(8,128)}, u32[]{:S(2)}) copy-start(f32[64,512]{1,0:T(8,128)} %get-tuple-element.90) | copy-start | bytes 393220
  202.4 3.0 %copy-start.2 = (f32[16,2048]{1,0:T(8,128)S(1)}, f32[16,2048]{1,0:T(8,128)}, u32[]{:S(2)}) copy-start(f32[16,2048]{1,0:T(8,128)} %get-tuple-element.91) | copy-start | bytes 393220
where the time goes:
time: 207 us; the launch traced here: 206 us
  Pallas kernels  184 us (89%)
  local copies, waits for them, and re-layouts  18.7 us (9%)
  other arithmetic  2.42 us (1%)
    pallas_call x1, Pallas kernels, body(): pl.pallas_call(functools.partial(reduce_kernel, n_entries), out_shape=tup...  74.6 us
    pallas_call x1, Pallas kernels, body(): pl.pallas_call(functools.partial(gather_kernel, n_entries), out_shape=tup...  74.4 us
    pallas_call x1, Pallas kernels, body(): pl.pallas_call(functools.partial(middle_kernel, tuple(ins) + tuple(outs)...  35.3 us
    unnamed x21, local copies, waits for them, and re-layouts  8.99 us

commit v1 on v0

v1 whole, which is shorter than its diff:
```python
import functools
import types

import jax
import jax.numpy as jnp
from jax import lax
from jax.experimental import pallas as pl
from jax.experimental.pallas import tpu as pltpu
from jax.sharding import PartitionSpec as P

HEADS = 8
HEAD = 64
PIECES = 7
LANES = 128
TBLOCK = 512
AXES = ("entries", "feat")
MESH = pl.DeviceIdType.MESH
VMEM = pltpu.VMEM
BF16 = jnp.bfloat16
F32 = jnp.float32

epsilon = 1e-05


def contract(left_side, right_side, left_dim, right_dim):
    return lax.dot_general(
        left_side,
        right_side,
        (((left_dim,), (right_dim,)), ((), ())),
        preferred_element_type=jnp.float32,
    )


class Place:
    def __init__(self, n_entries):
        entry = lax.axis_index("entries")
        self.n_z = n_entries // 4
        self.n = n_entries * 2
        self.y = lax.axis_index("feat")
        self.c = lax.rem(entry, 2)
        self.x = lax.rem(lax.div(entry, 2), 2)
        self.z = lax.div(entry, 4)
        self.line = entry * 2 + self.y
        first = self.c == 0
        self.x1 = jnp.where(first, 1 - self.x, self.x)
        self.y1 = jnp.where(first, self.y, 1 - self.y)
        self.x2 = jnp.where(first, self.x, 1 - self.x)
        self.y2 = jnp.where(first, 1 - self.y, self.y)

    def at(self, z, x, c, y):
        return ((z * 2 + x) * 2 + c, y)

    def along_z(self, step):
        return lax.rem(self.z + step, self.n_z)


def meet(place):
    p = place
    barrier = pltpu.get_barrier_semaphore()
    peers = [p.at(p.along_z(k), p.x, p.c, p.y) for k in range(1, p.n_z)]
    peers += [
        p.at(p.z, p.x, 1 - p.c, p.y),
        p.at(p.z, p.x1, p.c, p.y1),
        p.at(p.z, p.x2, p.c, p.y2),
    ]
    for peer in peers:
        pl.semaphore_signal(barrier, inc=1, device_id=peer, device_id_type=MESH)
    pl.semaphore_wait(barrier, len(peers))


def remote(src, dst, send, recv, to):
    return pltpu.make_async_remote_copy(
        src_ref=src, dst_ref=dst, send_sem=send, recv_sem=recv, device_id=to, device_id_type=MESH
    )


class Gather:
    def __init__(self, place, whole, send, recv):
        p = self.place = place
        nz = p.n_z
        self.nz = nz
        mine = whole.at[p.z, p.x, p.c, p.y]
        self.along = [
            remote(mine, mine, send.at[k - 1], recv.at[k - 1], p.at(p.along_z(k), p.x, p.c, p.y))
            for k in range(1, nz)
        ]
        col = [
            whole.at[:, p.x, p.c, p.y],
            whole.at[:, p.x1, p.c, p.y1],
            whole.at[:, p.x2, p.c, p.y2],
            whole.at[:, 1 - p.x, p.c, 1 - p.y],
        ]
        to_one = p.at(p.z, p.x1, p.c, p.y1)
        to_two = p.at(p.z, p.x2, p.c, p.y2)
        to_core = p.at(p.z, p.x, 1 - p.c, p.y)
        s = nz - 1
        self.one = remote(col[0], col[0], send.at[s], recv.at[s], to_one)
        self.two = remote(col[0], col[0], send.at[s + 1], recv.at[s + 1], to_two)
        self.three = remote(col[1], col[1], send.at[s + 2], recv.at[s + 2], to_two)
        self.core = [
            remote(col[k], col[k], send.at[s + 3 + k], recv.at[s + 3 + k], to_core)
            for k in range(4)
        ]

    def z_start(self):
        for copy in self.along:
            copy.start()

    def z_wait(self):
        for copy in self.along:
            copy.wait_recv()
        self.one.start()
        self.two.start()
        self.core[0].start()

    def one_wait(self):
        self.one.wait_recv()
        self.three.start()
        self.core[1].start()

    def two_wait(self):
        self.two.wait_recv()
        self.core[2].start()

    def three_wait(self):
        self.three.wait_recv()
        self.core[3].start()

    def core_wait(self):
        for copy in self.core:
            copy.wait_recv()

    def finish(self):
        for copy in self.along + [self.one, self.two, self.three] + self.core:
            copy.wait_send()


class Reduce:
    def __init__(self, place, parts, held_core, held_one, held_two, held_z, send, recv):
        p = self.place = place
        nz = p.n_z
        self.parts, self.held_core = parts, held_core
        self.held_one, self.held_two, self.held_z = held_one, held_two, held_z
        self.cols = [(p.x, p.y), (p.x1, p.y1), (p.x2, p.y2), (1 - p.x, 1 - p.y)]
        to_one = p.at(p.z, p.x1, p.c, p.y1)
        to_two = p.at(p.z, p.x2, p.c, p.y2)
        to_core = p.at(p.z, p.x, 1 - p.c, p.y)

        def col(k):
            return parts.at[:, self.cols[k][0], p.c, self.cols[k][1]]

        self.core = remote(parts.at[:, :, 1 - p.c], held_core, send.at[0], recv.at[0], to_core)
        self.one = [
            remote(col(1), held_one.at[0], send.at[1], recv.at[1], to_one),
            remote(col(3), held_one.at[1], send.at[2], recv.at[2], to_one),
        ]
        self.two = remote(col(2), held_two, send.at[3], recv.at[3], to_two)
        self.along = [
            remote(
                parts.at[p.along_z(k), p.x, p.c, p.y],
                held_z.at[k - 1],
                send.at[3 + k],
                recv.at[3 + k],
                p.at(p.along_z(k), p.x, p.c, p.y),
            )
            for k in range(1, nz)
        ]

    def add(self, k, other):
        p, (x, y) = self.place, self.cols[k]
        self.parts[:, x, p.c, y] = (
            self.parts[:, x, p.c, y].astype(F32) + other.astype(F32)
        ).astype(BF16)

    def core_start(self):
        self.core.start()

    def core_wait(self):
        self.core.wait_recv()
        for k in (3, 1, 2, 0):
            x, y = self.cols[k]
            self.add(k, self.held_core[:, x, y])
            if k == 3:
                self.one[1].start()
            if k == 1:
                self.one[0].start()

    def one_wait(self):
        self.one[1].wait_recv()
        self.add(2, self.held_one[1])
        self.two.start()
        self.one[0].wait_recv()
        self.add(0, self.held_one[0])

    def two_wait(self):
        self.two.wait_recv()
        self.add(0, self.held_two[...])
        for copy in self.along:
            copy.start()

    def z_wait(self, out):
        p = self.place
        total = self.parts[p.z, p.x, p.c, p.y].astype(F32)
        for k, copy in enumerate(self.along):
            copy.wait_recv()
            total = total + self.held_z[k].astype(F32)
        out[...] = total

    def finish(self):
        for copy in [self.core] + self.one + [self.two] + self.along:
            copy.wait_send()


def exchange(place, src, dst, send, recv):
    dst[place.line] = src[place.line]

    def begin(step, carry):
        other = lax.rem(place.line + step, place.n)
        remote(
            src.at[other],
            dst.at[place.line],
            send.at[step],
            recv.at[step],
            (lax.div(other, 2), lax.rem(other, 2)),
        ).start()
        return carry

    lax.fori_loop(1, place.n, begin, 0)


def exchange_wait(place, src, dst, send, recv, sends):
    def end(step, carry):
        other = lax.rem(place.line + step, place.n)
        copy = remote(
            src.at[other],
            dst.at[place.line],
            send.at[step],
            recv.at[step],
            (lax.div(other, 2), lax.rem(other, 2)),
        )
        if sends:
            copy.wait_send()
        else:
            copy.wait_recv()
        return carry

    lax.fori_loop(1, place.n, end, 0)


def text_keys(number, seg_rows, rows, segs, half, ids, mask, row_key, seg_key):
    length = ids.shape[0]
    entry = ids[...].reshape(1, length)
    source = ((entry.astype(F32) + 0.5) * (1.0 / number)).astype(jnp.int32)
    within = entry - source * number
    segment = jnp.zeros_like(entry)
    for h in range(1, segs):
        segment = segment + (within >= h * seg_rows).astype(jnp.int32)
    upper = (source >= half).astype(jnp.int32)
    row_key[...] = (source - half * upper) * rows + within - segment * seg_rows
    seg_key[...] = jnp.where(mask[...].reshape(1, length) != 0, upper * segs + segment, -1)


def text_blocks(length):
    whole = length // TBLOCK
    return whole, length - whole * TBLOCK


def one_hot(keys, depth):
    width = keys.shape[1]
    return (lax.broadcasted_iota(jnp.int32, (depth, width), 0) == keys).astype(F32).astype(BF16)


def scatter_block(start, width, row_ref, seg_ref, cot_ref, acc_ref):
    span = pl.ds(start, width)
    depth, side = acc_ref.shape[0], acc_ref.shape[1] // 2
    seg = seg_ref[:, span]
    cot = cot_ref[:, span].astype(F32)
    spread = jnp.concatenate(
        [jnp.where(seg == q, cot, 0.0).astype(BF16) for q in range(side // cot.shape[0])], axis=0
    )
    for k in range(2):
        hot = one_hot(row_ref[:, span] - k * depth, depth)
        acc_ref[:, k * side : (k + 1) * side] += contract(hot, spread, 1, 1)


class Sweep:
    def __init__(self, length, block):
        self.block, self.done = block, 0
        self.whole, self.tail = text_blocks(length)

    def go(self, count=None):
        low = self.done
        high = self.whole if count is None else min(self.whole, low + count)
        self.done = high

        def step(i, carry):
            self.block(pl.multiple_of(i * TBLOCK, TBLOCK), TBLOCK)
            return carry

        if high > low:
            lax.fori_loop(low, high, step, 0)
        if count is None and self.tail:
            self.block(self.whole * TBLOCK, self.tail)


def lookup_block(start, width, row_ref, seg_ref, table_ref, out_ref):
    span = pl.ds(start, width)
    hot = one_hot(row_ref[:, span], table_ref.shape[1])
    seg = seg_ref[:, span]
    wide = jnp.dot(table_ref[...], hot, preferred_element_type=F32)
    feats = out_ref.shape[0]
    found = jnp.zeros((feats, width), F32)
    for q in range(table_ref.shape[0] // feats):
        found = found + jnp.where(seg == q, wide[q * feats : (q + 1) * feats], 0.0)
    out_ref[:, span] = found.astype(BF16)


def cast_pair(value):
    high = value.astype(BF16)
    return high, (value - high.astype(F32)).astype(BF16)


def head_ones():
    head_row = lax.broadcasted_iota(jnp.int32, (4 * HEAD, 4 * HEAD), 0) // HEAD
    head_col = lax.broadcasted_iota(jnp.int32, (4 * HEAD, 4 * HEAD), 1) // HEAD
    return (head_row == head_col).astype(F32).astype(BF16)


def head_sum(value, ones):
    high, low = cast_pair(value)
    step = 4 * HEAD
    return jnp.concatenate(
        [
            jnp.dot(high[:, j : j + step], ones, preferred_element_type=F32)
            + jnp.dot(low[:, j : j + step], ones, preferred_element_type=F32)
            for j in range(0, value.shape[1], step)
        ],
        axis=1,
    )


def flat(ref, low=None, high=None):
    value = ref[...] if low is None else ref[:, :, :, :, :, low:high]
    return value.reshape(-1, value.shape[-1])


def spread_segments(blocks, feats, segs):
    lane = lax.broadcasted_iota(jnp.int32, blocks[0].shape, 1) // feats
    out = []
    for h in range(segs):
        whole = None
        for j in range(segs):
            shift = ((j - h) * feats) % LANES
            moved = blocks[j] if shift == 0 else pltpu.roll(blocks[j], shift, 1)
            whole = moved if whole is None else jnp.where(lane == j, moved, whole)
        out.append(whole)
    return out


class Block:
    def __init__(self, m, segs, seg_rows, rows, feats):
        self.m, self.segs, self.seg_rows, self.rows, self.feats = m, segs, seg_rows, rows, feats
        self.number = m.pieces.shape[1]
        self.width = m.pieces.shape[2]
        self.total = segs * rows

    def pieces_of(self, h):
        return min(self.seg_rows, max(self.number - h * self.seg_rows, 0))

    def column(self, ref):
        line = lax.broadcasted_iota(jnp.int32, (self.total, 1), 0)
        segment, within = line // self.rows, line % self.rows
        entry = jnp.where(within < self.seg_rows, segment * self.seg_rows + within, -1)
        values = ref[...].reshape(1, self.number)
        lane = lax.broadcasted_iota(jnp.int32, (self.total, self.number), 1)
        return jnp.sum(jnp.where(lane == entry, values, 0), axis=1, keepdims=True)

    def load(self):
        m = self.m
        m.length_col[...] = self.column(m.lengths)
        m.group_col[...] = self.column(m.groups)
        for p in range(PIECES):
            value = m.pieces[p].astype(F32)
            for h in range(self.segs):
                low, base, count = h * self.seg_rows, h * self.rows, self.pieces_of(h)
                m.unit[p, base : base + count, :] = value[low : low + count]
                m.unit[p, base + count : base + self.rows, :] = jnp.zeros(
                    (self.rows - count, self.width), F32
                )

    def norm_one(self):
        m, width = self.m, self.width
        small = flat(m.w_qkv, 3 * width, 3 * width + LANES).astype(F32).T
        m.small[...] = small[:8]
        start = m.unit[0]
        for g in range(m.n_groups):
            start = start + jnp.where(m.group_col[...] == g, small[2 + g : 3 + g, :], 0.0)
        m.unit[0] = start
        m.hidden[...] = start

        def one(p, carry):
            value = m.unit[p]
            centered = value - jnp.mean(value, axis=1, keepdims=True)
            inv = lax.rsqrt(jnp.mean(centered * centered, axis=1, keepdims=True) + epsilon)
            unit = centered * inv
            m.unit[p] = unit
            m.inv_one[p] = jnp.broadcast_to(inv, (self.total, LANES))
            m.normed[p] = (unit * m.small[0:1, :]).astype(BF16)
            return carry

        lax.fori_loop(0, PIECES, one, 0)

    def project_qkv(self):
        m, width = self.m, self.width
        step = 2 * LANES
        m.query[...] = jnp.dot(
            m.normed[0], flat(m.w_qkv, 0, width), preferred_element_type=F32
        ).astype(BF16)

        def one(j, carry):
            span = pl.ds(pl.multiple_of(j * step, step), step)
            source = pl.ds(pl.multiple_of(width + j * step, step), step)
            weight = m.w_qkv[:, :, :, :, :, source].reshape(width, step)
            m.key_value[:, :, span] = (
                jnp.dot(
                    m.normed[...].reshape(PIECES * self.total, width),
                    weight,
                    preferred_element_type=F32,
                )
                .astype(BF16)
                .reshape(PIECES, self.total, step)
            )
            return carry

        lax.fori_loop(0, 2 * width // step, one, 0)

    def attend(self):
        m, width = self.m, self.width
        ones = head_ones()

        def score(p, carry):
            product = m.query[...].astype(F32) * m.key_value[p, :, :width].astype(F32)
            m.prob[p] = head_sum(product, ones) * (HEAD**-0.5)
            return carry

        lax.fori_loop(0, PIECES, score, 0)

        def soft(i, carry):
            span = pl.ds(pl.multiple_of(i * 16, 16), 16)
            length = m.length_col[span, :]
            scores = [
                jnp.where(p < length, m.prob[p, span, :], -1e30) for p in range(PIECES)
            ]
            highest = functools.reduce(jnp.maximum, scores)
            raised = [jnp.exp(s - highest) for s in scores]
            inv = 1.0 / functools.reduce(jnp.add, raised)
            total = jnp.zeros((16, width), F32)
            for p in range(PIECES):
                prob = raised[p] * inv
                m.prob[p, span, :] = prob
                total = total + prob.astype(BF16).astype(F32) * m.key_value[
                    p, span, width:
                ].astype(F32)
            m.attended[span, :] = total.astype(BF16)
            return carry

        lax.fori_loop(0, self.total // 16, soft, 0)

    def norm_two(self):
        m, width = self.m, self.width
        hidden = m.hidden[...] + jnp.dot(
            m.attended[...], flat(m.w_out), preferred_element_type=F32
        )
        m.hidden[...] = hidden
        centered = hidden - jnp.mean(hidden, axis=1, keepdims=True)
        inv = lax.rsqrt(jnp.mean(centered * centered, axis=1, keepdims=True) + epsilon)
        unit = centered * inv
        m.unit_two[...] = unit
        m.inv_two[...] = jnp.broadcast_to(inv, (self.total, LANES))
        m.normed_two[...] = (unit * m.small[1:2, :]).astype(BF16)

    def up(self):
        m, step = self.m, 2 * LANES

        def one(j, carry):
            span = pl.ds(pl.multiple_of(j * step, step), step)
            weight = m.w_up[:, :, :, :, :, span].reshape(self.width, step)
            upward = jnp.dot(m.normed_two[...], weight, preferred_element_type=F32)
            normal = 0.5 * (1.0 + lax.erf(upward * (0.5**0.5)))
            m.activated[:, span] = (upward * normal).astype(BF16)
            m.slope[:, span] = normal + upward * (
                jnp.exp(-0.5 * upward * upward) * 0.3989422804014327
            )
            return carry

        lax.fori_loop(0, m.activated.shape[1] // step, one, 0)

    def down(self):
        m = self.m
        m.output[...] = (
            m.hidden[...]
            + jnp.dot(m.activated[...], flat(m.w_down), preferred_element_type=F32)
        ).astype(BF16)

    def table(self):
        m, segs, rows = self.m, self.segs, self.rows

        def one(g, carry):
            span = pl.ds(pl.multiple_of(g * LANES, LANES), LANES)
            weight = m.w_proj[:, :, :, :, :, span].reshape(self.width, LANES)
            value = jnp.dot(m.output[...], weight, preferred_element_type=F32)
            parts = [value[h * rows : (h + 1) * rows] for h in range(segs)]
            for j, part in enumerate(spread_segments(parts, self.feats, segs)):
                m.came_grad[g * segs + j] = part.astype(BF16)
            return carry

        lax.fori_loop(0, m.w_proj.shape[-1] // LANES, one, 0)


    def table_back(self):
        m, segs, rows = self.m, self.segs, self.rows

        def one(g, carry):
            span = pl.ds(pl.multiple_of(g * LANES, LANES), LANES)
            parts = [m.came_grad[g * segs + j].astype(F32) for j in range(segs)]
            for h, part in enumerate(spread_segments(parts, self.feats, segs)):
                m.grad_table[h * rows : (h + 1) * rows, span] = part.astype(BF16)
            return carry

        lax.fori_loop(0, m.grad_table.shape[1] // LANES, one, 0)

    def put(self, ref, value):
        ref[...] = value.astype(BF16).reshape(ref.shape)

    def proj_grad(self):
        m = self.m
        self.put(m.d_proj, contract(m.output[...], m.grad_table[...], 0, 0))

    def proj_back(self):
        m = self.m
        grad_output = contract(m.grad_table[...], flat(m.w_proj), 1, 1)
        m.grad_output[...] = grad_output
        m.grad_branch[...] = grad_output.astype(BF16)

    def down_grad(self):
        m = self.m
        self.put(m.d_down, contract(m.activated[...], m.grad_branch[...], 0, 0))

    def down_back(self):
        m = self.m
        grad_act = contract(m.grad_branch[...], flat(m.w_down), 1, 1)
        m.activated[...] = (grad_act * m.slope[...]).astype(BF16)

    def up_grad(self):
        m = self.m
        self.put(m.d_up, contract(m.normed_two[...], m.activated[...], 0, 0))

    def up_back(self):
        m = self.m
        grad = contract(m.activated[...], flat(m.w_up), 1, 1)
        m.d_small[...] = jnp.zeros_like(m.d_small)
        unit = m.unit_two[...]
        m.d_small[1:2, :] = jnp.sum(grad * unit, axis=0, keepdims=True)
        grad = grad * m.small[1:2, :]
        first = jnp.mean(grad, axis=1, keepdims=True)
        second = jnp.mean(grad * unit, axis=1, keepdims=True)
        hidden = m.grad_output[...] + m.inv_two[:, 0:1] * (grad - first - unit * second)
        m.hidden[...] = hidden
        m.grad_branch[...] = hidden.astype(BF16)

    def out_back(self):
        m = self.m
        self.put(m.d_out, contract(m.attended[...], m.grad_branch[...], 0, 0))
        m.attended[...] = contract(m.grad_branch[...], flat(m.w_out), 1, 1).astype(BF16)

    def attend_back(self):
        m, width = self.m, self.width
        ones = head_ones()
        scale = HEAD**-0.5

        def score(p, carry):
            product = m.attended[...].astype(F32) * m.key_value[p, :, width:].astype(F32)
            m.grad_prob[p] = head_sum(product, ones)
            return carry

        lax.fori_loop(0, PIECES, score, 0)

        def soft(i, carry):
            span = pl.ds(pl.multiple_of(i * 16, 16), 16)
            inner = jnp.zeros((16, width), F32)
            for p in range(PIECES):
                inner = inner + m.prob[p, span, :] * m.grad_prob[p, span, :]
            query = m.query[span, :].astype(F32)
            grad_att = m.attended[span, :].astype(F32)
            grad_query = jnp.zeros((16, width), F32)
            for p in range(PIECES):
                prob = m.prob[p, span, :]
                low = prob.astype(BF16).astype(F32)
                grad = (prob * (m.grad_prob[p, span, :] - inner)).astype(BF16).astype(F32)
                grad_query = grad_query + grad * m.key_value[p, span, :width].astype(F32)
                m.key_value[p, span, :width] = (grad * query * scale).astype(BF16)
                m.key_value[p, span, width:] = (low * grad_att).astype(BF16)
            m.query[span, :] = (grad_query * scale).astype(BF16)
            return carry

        lax.fori_loop(0, self.total // 16, soft, 0)

    def qkv_back(self):
        m, width = self.m, self.width
        lead = m.d_qkv.shape[:-1]
        step = 2 * LANES
        m.d_qkv[:, :, :, :, :, :width] = (
            contract(m.normed[0], m.query[...], 0, 0).astype(BF16).reshape(lead + (width,))
        )

        def one(j, carry):
            target = pl.ds(pl.multiple_of(width + j * step, step), step)
            span = pl.ds(pl.multiple_of(j * step, step), step)
            grad = m.key_value[:, :, span].reshape(PIECES * self.total, step)
            m.d_qkv[:, :, :, :, :, target] = (
                contract(m.normed[...].reshape(PIECES * self.total, width), grad, 0, 0)
                .astype(BF16)
                .reshape(lead + (step,))
            )
            return carry

        lax.fori_loop(0, 2 * width // step, one, 0)

    def normed_back(self):
        m, width = self.m, self.width
        m.grad_prob[...] = contract(
            m.key_value[...].reshape(PIECES * self.total, 2 * width),
            flat(m.w_qkv, width, 3 * width),
            1,
            1,
        ).reshape(PIECES, self.total, width)
        m.grad_prob[0] += contract(m.query[...], flat(m.w_qkv, 0, width), 1, 1)

    def norm_back(self):
        m, width = self.m, self.width
        gain = m.small[0:1, :]

        def back(p):
            grad = m.grad_prob[p]
            unit = m.unit[p]
            m.d_small[0:1, :] += jnp.sum(grad * unit, axis=0, keepdims=True)
            grad = grad * gain
            first = jnp.mean(grad, axis=1, keepdims=True)
            second = jnp.mean(grad * unit, axis=1, keepdims=True)
            grad = m.inv_one[p][:, 0:1] * (grad - first - unit * second)
            if p == 0:
                grad = grad + m.hidden[...]
                for g in range(m.n_groups):
                    m.d_small[2 + g : 3 + g, :] = jnp.sum(
                        jnp.where(m.group_col[...] == g, grad, 0.0), axis=0, keepdims=True
                    )
            for h in range(self.segs):
                low, base, count = h * self.seg_rows, h * self.rows, self.pieces_of(h)
                m.grad_output[low : low + count, :] = grad[base : base + count]
            m.grad_pieces[p] = m.grad_output[0 : self.number, :].astype(BF16)

        for p in range(PIECES):
            back(p)
        lead = m.d_qkv.shape[:-1]
        small = jnp.concatenate(
            [m.d_small[...], jnp.zeros((LANES - 8, width), F32)], axis=0
        ).T
        m.d_qkv[:, :, :, :, :, 3 * width :] = small.astype(BF16).reshape(lead + (LANES,))


def block_scratch(n, rows, total, width, hidden, out_width):
    return dict(
        length_col=((total, 1), jnp.int32),
        group_col=((total, 1), jnp.int32),
        unit=((PIECES, total, width), F32),
        inv_one=((PIECES, total, LANES), F32),
        small=((8, width), F32),
        normed=((PIECES, total, width), BF16),
        query=((total, width), BF16),
        key_value=((PIECES, total, 2 * width), BF16),
        prob=((PIECES, total, width), F32),
        attended=((total, width), BF16),
        hidden=((total, width), F32),
        unit_two=((total, width), F32),
        inv_two=((total, LANES), F32),
        normed_two=((total, width), BF16),
        activated=((total, hidden), BF16),
        slope=((total, hidden), F32),
        output=((total, width), BF16),
        grad_table=((total, out_width), BF16),
        grad_output=((total, width), F32),
        grad_branch=((total, width), BF16),
        d_small=((8, width), F32),
        grad_prob=((PIECES, total, width), F32),
    )


NAMES = ("qkv", "out", "up", "down", "proj")


def main_kernel(n_entries, names, segs, seg_rows, rows, *refs):
    m = types.SimpleNamespace(**dict(zip(names, refs)))
    place = Place(n_entries)
    n, half = place.n, place.n // 2
    shard = m.ln1_gain.shape[0]
    m.n_groups = m.group_table.shape[0]
    feats = m.grad_embed.shape[0]
    block = Block(m, segs, seg_rows, rows, feats)
    width = block.width
    gather, reduce = types.SimpleNamespace(), types.SimpleNamespace()
    for i, name in enumerate(NAMES):
        whole, parts = getattr(m, "w_" + name), getattr(m, "d_" + name)
        setattr(gather, name, Gather(place, whole, m.g_send.at[i], m.g_recv.at[i]))
        held = [getattr(m, f"{kind}_{name}") for kind in ("core", "one", "two", "along")]
        setattr(reduce, name, Reduce(place, parts, *held, m.r_send.at[i], m.r_recv.at[i]))
        if name != "qkv":
            whole[place.z, place.x, place.c, place.y] = getattr(m, "s_" + name)[...]
    mine = m.w_qkv.at[place.z, place.x, place.c, place.y]
    mine[:, : 3 * width] = m.s_qkv[...]
    small = jnp.concatenate(
        [
            m.ln1_gain[...].astype(F32).reshape(1, shard),
            m.ln2_gain[...].astype(F32).reshape(1, shard),
            m.group_table[...].astype(F32),
            jnp.zeros((6 - m.n_groups, shard), F32),
        ],
        axis=0,
    )
    small = jnp.concatenate([small, jnp.zeros((8, LANES - shard), F32)], axis=1).T
    small = jnp.concatenate([small[:shard], jnp.zeros((shard, LANES - 8), F32)], axis=1)
    mine[:, 3 * width :] = small.astype(BF16)
    meet(place)
    gather.out.z_start()
    gather.qkv.z_start()

    text_len = m.text_ids.shape[0]
    text_keys(
        block.number, seg_rows, rows, segs, half, m.text_ids, m.text_mask, m.row_key, m.seg_key
    )
    acc = m.grad_prob.reshape(PIECES * block.total, width)
    acc = acc.at[pl.ds(0, half * rows // 2), pl.ds(0, 4 * LANES)]
    acc[...] = jnp.zeros(acc.shape, F32)
    scatter = Sweep(
        text_len,
        lambda start, count: scatter_block(
            start, count, m.row_key, m.seg_key, m.grad_embed, acc
        ),
    )
    scatter.go(2)
    gather.out.z_wait()
    gather.up.z_start()
    scatter.go(3)
    gather.qkv.z_wait()
    block.load()
    gather.out.one_wait()
    gather.out.two_wait()
    scatter.go(3)
    gather.out.three_wait()
    gather.qkv.one_wait()
    gather.down.z_start()
    scatter.go(3)
    gather.qkv.two_wait()
    gather.up.z_wait()
    gather.proj.z_start()
    scatter.go(3)
    gather.qkv.three_wait()
    gather.out.core_wait()
    scatter.go()

    def pack(i, carry):
        span = pl.ds(pl.multiple_of(i * rows, rows), rows)
        for k in range(4):
            value = acc[span, k * LANES : (k + 1) * LANES]
            m.sent_grad[i + (k // 2) * (half // 2) + (k % 2) * half] = value.astype(BF16)
        return carry

    lax.fori_loop(0, half // 2, pack, 0)
    gather.qkv.core_wait()
    block.norm_one()
    gather.up.one_wait()
    gather.up.two_wait()
    block.project_qkv()
    gather.down.z_wait()
    exchange(place, m.sent_grad, m.came_grad, m.xg_send, m.xg_recv)
    gather.up.three_wait()
    block.attend()
    block.norm_two()
    gather.down.one_wait()
    gather.down.two_wait()
    gather.up.core_wait()
    block.up()
    gather.proj.z_wait()
    gather.down.three_wait()
    gather.proj.one_wait()
    gather.proj.two_wait()
    gather.down.core_wait()
    block.down()
    exchange_wait(place, m.sent_grad, m.came_grad, m.xg_send, m.xg_recv, False)
    block.table_back()
    block.proj_grad()
    reduce.proj.core_start()
    gather.proj.three_wait()
    reduce.proj.core_wait()
    gather.proj.core_wait()
    block.proj_back()
    block.down_grad()
    reduce.down.core_start()
    block.table()
    exchange(place, m.came_grad, m.came_table, m.xt_send, m.xt_recv)
    block.down_back()
    block.up_grad()
    reduce.up.core_start()
    reduce.down.core_wait()
    block.up_back()
    block.out_back()
    reduce.out.core_start()
    reduce.proj.one_wait()
    block.attend_back()
    reduce.up.core_wait()
    block.qkv_back()
    reduce.proj.two_wait()
    block.normed_back()
    reduce.down.one_wait()
    block.norm_back()
    reduce.qkv.core_start()
    pieces_out = pltpu.make_async_copy(m.grad_pieces, m.o_pieces, m.o_sem.at[0])
    pieces_out.start()
    reduce.qkv.core_wait()
    reduce.down.two_wait()
    exchange_wait(place, m.came_grad, m.came_table, m.xt_send, m.xt_recv, False)
    for side in range(2):
        part = m.came_table[side * half : (side + 1) * half].reshape(half * rows, LANES)
        m.table[side * LANES : (side + 1) * LANES, :] = part.astype(F32).T.astype(BF16)
    lookup = Sweep(
        text_len,
        lambda start, count: lookup_block(
            start, count, m.row_key, m.seg_key, m.table, m.found
        ),
    )
    outs = []

    def finish(i, name):
        stage = getattr(m, "t_" + name)
        getattr(reduce, name).z_wait(stage)
        source = stage.at[:, : 3 * width] if name == "qkv" else stage
        outs.append(pltpu.make_async_copy(source, getattr(m, "o_" + name), m.o_sem.at[i]))
        outs[-1].start()

    lookup.go(3)
    reduce.up.one_wait()
    lookup.go(2)
    finish(1, "proj")
    lookup.go(2)
    reduce.out.core_wait()
    reduce.up.two_wait()
    lookup.go(2)
    reduce.qkv.one_wait()
    lookup.go(2)
    finish(2, "down")
    lookup.go(2)
    reduce.qkv.two_wait()
    lookup.go(2)
    reduce.out.one_wait()
    finish(3, "up")
    lookup.go()
    found_out = pltpu.make_async_copy(m.found, m.o_found, m.o_sem.at[4])
    found_out.start()
    reduce.out.two_wait()
    finish(5, "qkv")
    small = m.t_qkv[:, 3 * width :]
    small = jnp.concatenate([small, jnp.zeros((LANES - shard, LANES), F32)], axis=0).T
    m.o_ln1[...] = small[0:1, :shard].reshape(shard)
    m.o_ln2[...] = small[1:2, :shard].reshape(shard)
    m.o_group[...] = small[2 : 2 + m.n_groups, :shard]
    finish(6, "out")
    exchange_wait(place, m.sent_grad, m.came_grad, m.xg_send, m.xg_recv, True)
    exchange_wait(place, m.came_grad, m.came_table, m.xt_send, m.xt_recv, True)
    for name in NAMES:
        getattr(gather, name).finish()
        getattr(reduce, name).finish()
    pieces_out.wait()
    found_out.wait()
    for copy in outs:
        copy.wait()


def copy_kernel(count, *refs):
    ins, outs, held = refs[:count], refs[count : 2 * count], refs[2 * count : 3 * count]
    come, go = refs[3 * count :]
    inward = [pltpu.make_async_copy(ins[i], held[i], come.at[i]) for i in range(count)]
    outward = [pltpu.make_async_copy(held[i], outs[i], go.at[i]) for i in range(count)]
    for copy in inward:
        copy.start()
    for i in range(count):
        inward[i].wait()
        outward[i].start()
    for copy in outward:
        copy.wait()


def full(shape, dtype):
    return jax.ShapeDtypeStruct(shape, dtype)


def body(
    mesh_shape,
    pieces,
    lengths,
    entry_group,
    group_table,
    ln1_gain,
    w_qkv,
    w_out,
    ln2_gain,
    w_up,
    w_down,
    w_proj,
    text_ids,
    text_mask,
    grad_embed,
):
    n_entries = mesh_shape["entries"]
    n = n_entries * mesh_shape["feat"]
    n_z = n_entries // 4
    number, width = pieces.shape[0], pieces.shape[2]
    feats = grad_embed.shape[0]
    text_len = text_ids.shape[0]
    segs = LANES // feats
    seg_rows = -(-number // segs)
    rows = -(-seg_rows // 16) * 16
    half, total = n // 2, segs * rows
    pieces = jnp.transpose(pieces, (1, 0, 2))
    vmem = pl.BlockSpec(memory_space=VMEM)
    hbm = pl.BlockSpec(memory_space=pl.ANY)
    dma = pltpu.SemaphoreType.DMA

    ins = dict(
        pieces=pieces,
        lengths=lengths,
        groups=entry_group,
        group_table=group_table,
        ln1_gain=ln1_gain,
        s_qkv=w_qkv,
        s_out=w_out,
        ln2_gain=ln2_gain,
        s_up=w_up,
        s_down=w_down,
        s_proj=w_proj,
        text_ids=text_ids,
        text_mask=text_mask,
        grad_embed=grad_embed,
    )
    outs = dict(
        o_found=full((feats, text_len), BF16),
        o_pieces=full(pieces.shape, BF16),
        o_group=full(group_table.shape, F32),
        o_ln1=full(ln1_gain.shape, F32),
        o_qkv=full(w_qkv.shape, F32),
        o_out=full(w_out.shape, F32),
        o_ln2=full(ln2_gain.shape, F32),
        o_up=full(w_up.shape, F32),
        o_down=full(w_down.shape, F32),
        o_proj=full(w_proj.shape, F32),
    )
    tiny = ("o_group", "o_ln1", "o_ln2")
    scratch = {
        name: VMEM(*item)
        for name, item in block_scratch(
            n, rows, total, width, w_up.shape[1], w_proj.shape[1]
        ).items()
    }
    lead = (n_z, 2, 2, 2)
    shapes = dict(
        qkv=(w_qkv.shape[0], w_qkv.shape[1] + LANES),
        out=w_out.shape,
        up=w_up.shape,
        down=w_down.shape,
        proj=w_proj.shape,
    )
    for name, shape in shapes.items():
        scratch["w_" + name] = VMEM(lead + shape, BF16)
        scratch["d_" + name] = VMEM(lead + shape, BF16)
        scratch["t_" + name] = VMEM(shape, F32)
        scratch["core_" + name] = VMEM((n_z, 2, 2) + shape, BF16)
        scratch["one_" + name] = VMEM((2, n_z) + shape, BF16)
        scratch["two_" + name] = VMEM((n_z,) + shape, BF16)
        scratch["along_" + name] = VMEM((n_z - 1,) + shape, BF16)
    for name in ("sent_grad", "came_grad", "came_table"):
        scratch[name] = VMEM((n, rows, LANES), BF16)
    scratch.update(
        row_key=VMEM((1, text_len), jnp.int32),
        seg_key=VMEM((1, text_len), jnp.int32),
        table=VMEM((2 * LANES, half * rows), BF16),
        found=VMEM((feats, text_len), BF16),
        grad_pieces=VMEM(pieces.shape, BF16),
        g_send=dma((len(NAMES), n_z + 6)),
        g_recv=dma((len(NAMES), n_z + 6)),
        r_send=dma((len(NAMES), n_z + 4)),
        r_recv=dma((len(NAMES), n_z + 4)),
        xg_send=dma((n,)),
        xg_recv=dma((n,)),
        xt_send=dma((n,)),
        xt_recv=dma((n,)),
        o_sem=dma((7,)),
    )
    results = pl.pallas_call(
        functools.partial(
            main_kernel,
            n_entries,
            tuple(ins) + tuple(outs) + tuple(scratch),
            segs,
            seg_rows,
            rows,
        ),
        out_shape=tuple(outs.values()),
        in_specs=[vmem] * len(ins),
        out_specs=tuple(vmem if name in tiny else hbm for name in outs),
        scratch_shapes=list(scratch.values()),
        compiler_params=pltpu.CompilerParams(
            collective_id=0, has_side_effects=True, vmem_limit_bytes=VMEM_BYTES
        ),
    )(*ins.values())
    results = pl.pallas_call(
        functools.partial(copy_kernel, len(results)),
        out_shape=tuple(outs.values()),
        in_specs=[hbm] * len(results),
        out_specs=(hbm,) * len(results),
        scratch_shapes=[VMEM(leaf.shape, leaf.dtype) for leaf in outs.values()]
        + [dma((len(results),)), dma((len(results),))],
    )(*results)
    found, grad_pieces, *others = results
    return (found, jnp.transpose(grad_pieces, (1, 0, 2)), *others)


VMEM_BYTES = 63 * 2**20


def solution(mesh):
    both = P(AXES)
    rows = P(AXES, None)
    return jax.shard_map(
        functools.partial(body, dict(mesh.shape)),
        mesh=mesh,
        in_specs=(
            P(AXES, None, None),
            both,
            both,
            P(None, AXES),
            both,
            rows,
            rows,
            both,
            rows,
            rows,
            rows,
            P(),
            P(),
            rows,
        ),
        out_specs=(
            rows,
            P(AXES, None, None),
            P(None, AXES),
            both,
            rows,
            rows,
            both,
            rows,
            rows,
            rows,
        ),
        check_vma=False,
    )
```

time: 207 us -> 131 us (0.63)
  Pallas kernels: 184 us -> 130 us
  local copies, waits for them, and re-layouts: 18.7 us -> 0 us
  other arithmetic: 2.42 us -> 0 us
    pallas_call x3 -> x2, Pallas kernels: 184 us -> 130 us  [the longest x1 127 us: body(): pl.pallas_call(functools.partial(main_kernel, n_entries, tuple(ins) + tup...]
    unnamed x21 -> x0, local copies, waits for them, and re-layouts: 8.99 us -> none
    reshape x4 -> x0, local copies, waits for them, and re-layouts: 3.1 us -> none  [the longest x2 1.58 us: column(): return jnp.pad(values, ((0, 0), (0, rows - seg_rows))).reshape(total, 1)]
    slice x2 -> x0, local copies, waits for them, and re-layouts: 3.05 us -> none  [the longest x1 1.54 us: body(): s_qkv[:, :3 * width]]
    broadcast_in_dim x4 -> x0, local copies, waits for them, and re-layouts: 2.77 us -> none  [the longest x2 1.28 us: body(): row_key, seg_key = (row_key[None, :], seg_key[None, :])]
where the time goes in v1:
time: 131 us
  Pallas kernels  130 us (99%)
    pallas_call x1, Pallas kernels, body(): pl.pallas_call(functools.partial(main_kernel, n_entries, tuple(ins) + tup...  127 us
    pallas_call x1, Pallas kernels, body(): pl.pallas_call(functools.partial(copy_kernel, len(results)), out_shape=tu...  3.01 us

profile of v1, /device:TPU:0, one launch (start us, length us, event | category | flops | bytes accessed | tf_op | source)
XLA Modules:
  0.0 130.8 jit_solution(13788654467945993553)
XLA Ops:
  0.6 126.9 %shard_map.213 = (bf16[64,9344]{1,0:T(8,128)(2,1)}, bf16[7,146,512]{2,1,0:T(8,128)(2,1)}, f32[4,16]{1,0:T(4,128)}, f32[16]{0:T(128)}, f32[16,1536]{1,0:T(8,128)}...) custom-call(bf16[7,146,512]{2,1,0:T(8,128)(2,1)} %bitcast.2, ...), custom_call_target="tpu_custom_call" | custom-call | tf_op jit(solution)/shard_map/pallas_call | solution.py:1006
  127.6 3.0 %shard_map.214 = (bf16[64,9344]{1,0:T(8,128)(2,1)}, bf16[7,146,512]{2,1,0:T(8,128)(2,1)}, f32[4,16]{1,0:T(4,128)}, f32[16]{0:T(128)}, f32[16,1536]{1,0:T(8,128)}...) custom-call(bf16[64,9344]{1,0:T(8,128)(2,1)} %get-tuple-element.30.refs_0_,, ...), custom_call_target="tpu_custom_call" | custom-call | tf_op jit(solution)/shard_map/pallas_call | solution.py:1023

commit v2 on v1

--- a/solution.py
+++ b/solution.py
@@ -54,85 +54,91 @@
         return lax.rem(self.z + step, self.n_z)
 
 
-def meet(place):
+def partners(place):
     p = place
-    barrier = pltpu.get_barrier_semaphore()
-    peers = [p.at(p.along_z(k), p.x, p.c, p.y) for k in range(1, p.n_z)]
-    peers += [
+    return [p.at(p.along_z(k), p.x, p.c, p.y) for k in range(1, p.n_z)] + [
         p.at(p.z, p.x, 1 - p.c, p.y),
         p.at(p.z, p.x1, p.c, p.y1),
         p.at(p.z, p.x2, p.c, p.y2),
     ]
-    for peer in peers:
-        pl.semaphore_signal(barrier, inc=1, device_id=peer, device_id_type=MESH)
-    pl.semaphore_wait(barrier, len(peers))
 
 
 def remote(src, dst, send, recv, to):
     return pltpu.make_async_remote_copy(
         src_ref=src, dst_ref=dst, send_sem=send, recv_sem=recv, device_id=to, device_id_type=MESH
     )
+
+
+def thirds(n_z):
+    others = list(range(1, n_z))
+    return [others[i * len(others) // 3 : (i + 1) * len(others) // 3] for i in range(3)]
 
 
 class Gather:
     def __init__(self, place, whole, send, recv):
         p = self.place = place
         nz = p.n_z
-        self.nz = nz
-        mine = whole.at[p.z, p.x, p.c, p.y]
-        self.along = [
-            remote(mine, mine, send.at[k - 1], recv.at[k - 1], p.at(p.along_z(k), p.x, p.c, p.y))
-            for k in range(1, nz)
-        ]
-        col = [
-            whole.at[:, p.x, p.c, p.y],
-            whole.at[:, p.x1, p.c, p.y1],
-            whole.at[:, p.x2, p.c, p.y2],
-            whole.at[:, 1 - p.x, p.c, 1 - p.y],
-        ]
+        self.groups = thirds(nz)
         to_one = p.at(p.z, p.x1, p.c, p.y1)
         to_two = p.at(p.z, p.x2, p.c, p.y2)
         to_core = p.at(p.z, p.x, 1 - p.c, p.y)
-        s = nz - 1
-        self.one = remote(col[0], col[0], send.at[s], recv.at[s], to_one)
-        self.two = remote(col[0], col[0], send.at[s + 1], recv.at[s + 1], to_two)
-        self.three = remote(col[1], col[1], send.at[s + 2], recv.at[s + 2], to_two)
-        self.core = [
-            remote(col[k], col[k], send.at[s + 3 + k], recv.at[s + 3 + k], to_core)
-            for k in range(4)
-        ]
-
-    def z_start(self):
-        for copy in self.along:
+
+        def shard(k, x, y):
+            return whole.at[p.along_z(nz - k), x, p.c, y]
+
+        def copy(ref, index, to):
+            return remote(ref, ref, send, recv.at[index], to)
+
+        self.along = {
+            k: copy(shard(0, p.x, p.y), k - 1, p.at(p.along_z(k), p.x, p.c, p.y))
+            for k in range(1, nz)
+        }
+        self.one = [copy(shard(k, p.x, p.y), nz - 1 + k, to_one) for k in range(nz)]
+        base = 2 * nz - 1
+        self.two = [copy(shard(k, p.x, p.y), base, to_two) for k in range(nz)]
+        self.three = [copy(shard(k, p.x1, p.y1), base + 1, to_two) for k in range(nz)]
+        cols = [(p.x, p.y), (p.x1, p.y1), (p.x2, p.y2), (1 - p.x, 1 - p.y)]
+        self.core = [copy(whole.at[:, x, p.c, y], base + 2, to_core) for x, y in cols]
+        self.all_two = copy(whole.at[:, p.x, p.c, p.y], base, to_two)
+        self.all_three = copy(whole.at[:, p.x1, p.c, p.y1], base + 1, to_two)
+        self.all_core = copy(whole.at[:, :, p.c], base + 2, to_core)
+        lines = whole.reshape((p.n,) + whole.shape[4:])
+        self.all_sent = copy(lines.at[pl.ds(0, p.n - 1)], base, to_two)
+
+    def start(self):
+        for copy in self.along.values():
             copy.start()
-
-    def z_wait(self):
-        for copy in self.along:
-            copy.wait_recv()
-        self.one.start()
-        self.two.start()
-        self.core[0].start()
-
-    def one_wait(self):
-        self.one.wait_recv()
-        self.three.start()
-        self.core[1].start()
+        self.one[0].start()
+        self.two[0].start()
+
+    def z_wait(self, i):
+        for k in self.groups[i]:
+            self.along[k].wait_recv()
+            self.one[k].start()
+            self.two[k].start()
+        if i == 2:
+            self.core[0].start()
+
+    def one_wait(self, i):
+        for k in [0] if i == 0 else self.groups[i - 1]:
+            self.one[k].wait_recv()
+            self.three[k].start()
+        if i == 3:
+            self.core[1].start()
 
     def two_wait(self):
-        self.two.wait_recv()
+        self.all_two.wait_recv()
         self.core[2].start()
 
     def three_wait(self):
-        self.three.wait_recv()
+        self.all_three.wait_recv()
         self.core[3].start()
 
     def core_wait(self):
-        for copy in self.core:
-            copy.wait_recv()
+        self.all_core.wait_recv()
 
     def finish(self):
-        for copy in self.along + [self.one, self.two, self.three] + self.core:
-            copy.wait_send()
+        self.all_sent.wait_send()
 
 
 class Reduce:
@@ -149,22 +155,27 @@
         def col(k):
             return parts.at[:, self.cols[k][0], p.c, self.cols[k][1]]
 
-        self.core = remote(parts.at[:, :, 1 - p.c], held_core, send.at[0], recv.at[0], to_core)
+        self.core = remote(parts.at[:, :, 1 - p.c], held_core, send, recv.at[0], to_core)
         self.one = [
-            remote(col(1), held_one.at[0], send.at[1], recv.at[1], to_one),
-            remote(col(3), held_one.at[1], send.at[2], recv.at[2], to_one),
+            remote(col(1), held_one.at[0], send, recv.at[1], to_one),
+            remote(col(3), held_one.at[1], send, recv.at[2], to_one),
         ]
-        self.two = remote(col(2), held_two, send.at[3], recv.at[3], to_two)
+        self.two = remote(col(2), held_two, send, recv.at[3], to_two)
         self.along = [
             remote(
                 parts.at[p.along_z(k), p.x, p.c, p.y],
                 held_z.at[k - 1],
-                send.at[3 + k],
-                recv.at[3 + k],
+                send,
+                recv.at[4],
                 p.at(p.along_z(k), p.x, p.c, p.y),
             )
             for k in range(1, nz)
         ]
+
+        landed = held_z.at[pl.ds(0, nz - 1)]
+        self.all_along = remote(landed, landed, send, recv.at[4], to_two)
+        lines = parts.reshape((p.n,) + parts.shape[4:]).at[pl.ds(0, p.n - 1)]
+        self.all_sent = remote(lines, lines, send, recv.at[4], to_two)
 
     def add(self, k, other):
         p, (x, y) = self.place, self.cols[k]
@@ -189,6 +200,8 @@
         self.one[1].wait_recv()
         self.add(2, self.held_one[1])
         self.two.start()
+
+    def one_more_wait(self):
         self.one[0].wait_recv()
         self.add(0, self.held_one[0])
 
@@ -201,14 +214,13 @@
     def z_wait(self, out):
         p = self.place
         total = self.parts[p.z, p.x, p.c, p.y].astype(F32)
-        for k, copy in enumerate(self.along):
-            copy.wait_recv()
+        self.all_along.wait_recv()
+        for k in range(len(self.along)):
             total = total + self.held_z[k].astype(F32)
         out[...] = total
 
     def finish(self):
-        for copy in [self.core] + self.one + [self.two] + self.along:
-            copy.wait_send()
+        self.all_sent.wait_send()
 
 
 def exchange(place, src, dst, send, recv):
@@ -216,35 +228,23 @@
 
     def begin(step, carry):
         other = lax.rem(place.line + step, place.n)
-        remote(
-            src.at[other],
-            dst.at[place.line],
-            send.at[step],
-            recv.at[step],
-            (lax.div(other, 2), lax.rem(other, 2)),
-        ).start()
+        to = (lax.div(other, 2), lax.rem(other, 2))
+        remote(src.at[other], dst.at[place.line], send, recv, to).start()
         return carry
 
     lax.fori_loop(1, place.n, begin, 0)
 
 
 def exchange_wait(place, src, dst, send, recv, sends):
-    def end(step, carry):
-        other = lax.rem(place.line + step, place.n)
-        copy = remote(
-            src.at[other],
-            dst.at[place.line],
-            send.at[step],
-            recv.at[step],
-            (lax.div(other, 2), lax.rem(other, 2)),
-        )
-        if sends:
-            copy.wait_send()
-        else:
-            copy.wait_recv()
-        return carry
-
-    lax.fori_loop(1, place.n, end, 0)
+    blocks = pl.ds(0, place.n - 1)
+    other = lax.rem(place.line + 1, place.n)
+    copy = remote(
+        src.at[blocks], dst.at[blocks], send, recv, (lax.div(other, 2), lax.rem(other, 2))
+    )
+    if sends:
+        copy.wait_send()
+    else:
+        copy.wait_recv()
 
 
 def text_keys(number, seg_rows, rows, segs, half, ids, mask, row_key, seg_key):
@@ -288,10 +288,9 @@
         self.block, self.done = block, 0
         self.whole, self.tail = text_blocks(length)
 
-    def go(self, count=None):
-        low = self.done
-        high = self.whole if count is None else min(self.whole, low + count)
-        self.done = high
+    def go(self, low, high):
+        last = high == SHARES
+        low, high = low * self.whole // SHARES, high * self.whole // SHARES
 
         def step(i, carry):
             self.block(pl.multiple_of(i * TBLOCK, TBLOCK), TBLOCK)
@@ -299,7 +298,7 @@
 
         if high > low:
             lax.fori_loop(low, high, step, 0)
-        if count is None and self.tail:
+        if last and self.tail:
             self.block(self.whole * TBLOCK, self.tail)
 
 
@@ -390,7 +389,7 @@
 
     def norm_one(self):
         m, width = self.m, self.width
-        small = flat(m.w_qkv, 3 * width, 3 * width + LANES).astype(F32).T
+        small = flat(m.w_out, width, width + LANES).astype(F32).T
         m.small[...] = small[:8]
         start = m.unit[0]
         for g in range(m.n_groups):
@@ -410,31 +409,25 @@
 
         lax.fori_loop(0, PIECES, one, 0)
 
-    def project_qkv(self):
+    def project_qkv(self, i):
         m, width = self.m, self.width
-        step = 2 * LANES
-        m.query[...] = jnp.dot(
-            m.normed[0], flat(m.w_qkv, 0, width), preferred_element_type=F32
-        ).astype(BF16)
-
-        def one(j, carry):
-            span = pl.ds(pl.multiple_of(j * step, step), step)
-            source = pl.ds(pl.multiple_of(width + j * step, step), step)
-            weight = m.w_qkv[:, :, :, :, :, source].reshape(width, step)
-            m.key_value[:, :, span] = (
-                jnp.dot(
-                    m.normed[...].reshape(PIECES * self.total, width),
-                    weight,
-                    preferred_element_type=F32,
-                )
-                .astype(BF16)
-                .reshape(PIECES, self.total, step)
+        step = width // 2
+        if i == 4:
+            m.query[...] = jnp.dot(
+                m.normed[0], flat(m.w_qkv, 0, width), preferred_element_type=F32
+            ).astype(BF16)
+            return
+        m.key_value[:, :, i * step : (i + 1) * step] = (
+            jnp.dot(
+                m.normed[...].reshape(PIECES * self.total, width),
+                flat(m.w_qkv, width + i * step, width + (i + 1) * step),
+                preferred_element_type=F32,
             )
-            return carry
-
-        lax.fori_loop(0, 2 * width // step, one, 0)
-
-    def attend(self):
+            .astype(BF16)
+            .reshape(PIECES, self.total, step)
+        )
+
+    def score(self, i):
         m, width = self.m, self.width
         ones = head_ones()
 
@@ -443,7 +436,13 @@
             m.prob[p] = head_sum(product, ones) * (HEAD**-0.5)
             return carry
 
-        lax.fori_loop(0, PIECES, score, 0)
+        lax.fori_loop(*self.half_of(PIECES, i), score, 0)
+
+    def half_of(self, count, i):
+        return i * count // 2, (i + 1) * count // 2
+
+    def soft(self, half):
+        m, width = self.m, self.width
 
         def soft(i, carry):
             span = pl.ds(pl.multiple_of(i * 16, 16), 16)
@@ -464,12 +463,12 @@
             m.attended[span, :] = total.astype(BF16)
             return carry
 
-        lax.fori_loop(0, self.total // 16, soft, 0)
+        lax.fori_loop(*self.half_of(self.total // 16, half), soft, 0)
 
     def norm_two(self):
         m, width = self.m, self.width
         hidden = m.hidden[...] + jnp.dot(
-            m.attended[...], flat(m.w_out), preferred_element_type=F32
+            m.attended[...], flat(m.w_out, 0, width), preferred_element_type=F32
         )
         m.hidden[...] = hidden
         centered = hidden - jnp.mean(hidden, axis=1, keepdims=True)
@@ -479,8 +478,9 @@
         m.inv_two[...] = jnp.broadcast_to(inv, (self.total, LANES))
         m.normed_two[...] = (unit * m.small[1:2, :]).astype(BF16)
 
-    def up(self):
+    def up(self, i):
         m, step = self.m, 2 * LANES
+        tiles = m.activated.shape[1] // step
 
         def one(j, carry):
             span = pl.ds(pl.multiple_of(j * step, step), step)
@@ -493,7 +493,7 @@
             )
             return carry
 
-        lax.fori_loop(0, m.activated.shape[1] // step, one, 0)
+        lax.fori_loop(i * tiles // 4, (i + 1) * tiles // 4, one, 0)
 
     def down(self):
         m = self.m
@@ -502,23 +502,24 @@
             + jnp.dot(m.activated[...], flat(m.w_down), preferred_element_type=F32)
         ).astype(BF16)
 
-    def table(self):
+    def table(self, i):
         m, segs, rows = self.m, self.segs, self.rows
-
-        def one(g, carry):
-            span = pl.ds(pl.multiple_of(g * LANES, LANES), LANES)
-            weight = m.w_proj[:, :, :, :, :, span].reshape(self.width, LANES)
-            value = jnp.dot(m.output[...], weight, preferred_element_type=F32)
+        step = m.w_proj.shape[-1] // 4
+        wide = jnp.dot(
+            m.output[...],
+            flat(m.w_proj, i * step, (i + 1) * step),
+            preferred_element_type=F32,
+        )
+        for g in range(step // LANES):
+            value = wide[:, g * LANES : (g + 1) * LANES]
             parts = [value[h * rows : (h + 1) * rows] for h in range(segs)]
             for j, part in enumerate(spread_segments(parts, self.feats, segs)):
-                m.came_grad[g * segs + j] = part.astype(BF16)
-            return carry
-
-        lax.fori_loop(0, m.w_proj.shape[-1] // LANES, one, 0)
-
-
-    def table_back(self):
+                m.came_grad[i * (step // self.feats) + g * segs + j] = part.astype(BF16)
+
+
+    def table_back(self, i):
         m, segs, rows = self.m, self.segs, self.rows
+        groups = m.grad_table.shape[1] // LANES
 
         def one(g, carry):
             span = pl.ds(pl.multiple_of(g * LANES, LANES), LANES)
@@ -527,14 +528,19 @@
                 m.grad_table[h * rows : (h + 1) * rows, span] = part.astype(BF16)
             return carry
 
-        lax.fori_loop(0, m.grad_table.shape[1] // LANES, one, 0)
+        lax.fori_loop(*self.half_of(groups, i), one, 0)
 
     def put(self, ref, value):
         ref[...] = value.astype(BF16).reshape(ref.shape)
 
-    def proj_grad(self):
+    def halves(self, value, i):
+        half = value.shape[-1] // 2
+        return value[:, i * half : (i + 1) * half]
+
+    def proj_grad(self, i):
         m = self.m
-        self.put(m.d_proj, contract(m.output[...], m.grad_table[...], 0, 0))
+        target = (m.d_proj0, m.d_proj1)[i]
+        self.put(target, contract(m.output[...], self.halves(m.grad_table, i), 0, 0))
 
     def proj_back(self):
         m = self.m
@@ -542,18 +548,20 @@
         m.grad_output[...] = grad_output
         m.grad_branch[...] = grad_output.astype(BF16)
 
-    def down_grad(self):
+    def down_grad(self, i):
         m = self.m
-        self.put(m.d_down, contract(m.activated[...], m.grad_branch[...], 0, 0))
+        target = (m.d_down0, m.d_down1)[i]
+        self.put(target, contract(m.activated[...], self.halves(m.grad_branch, i), 0, 0))
 
     def down_back(self):
         m = self.m
         grad_act = contract(m.grad_branch[...], flat(m.w_down), 1, 1)
         m.activated[...] = (grad_act * m.slope[...]).astype(BF16)
 
-    def up_grad(self):
+    def up_grad(self, i):
         m = self.m
-        self.put(m.d_up, contract(m.normed_two[...], m.activated[...], 0, 0))
+        target = (m.d_up0, m.d_up1)[i]
+        self.put(target, contract(m.normed_two[...], self.halves(m.activated, i), 0, 0))
 
     def up_back(self):
         m = self.m
@@ -569,21 +577,28 @@
         m.grad_branch[...] = hidden.astype(BF16)
 
     def out_back(self):
-        m = self.m
-        self.put(m.d_out, contract(m.attended[...], m.grad_branch[...], 0, 0))
-        m.attended[...] = contract(m.grad_branch[...], flat(m.w_out), 1, 1).astype(BF16)
-
-    def attend_back(self):
+        m, width = self.m, self.width
+        m.d_out[:, :, :, :, :, :width] = (
+            contract(m.attended[...], m.grad_branch[...], 0, 0)
+            .astype(BF16)
+            .reshape(m.d_out.shape[:-1] + (width,))
+        )
+        m.attended[...] = contract(m.grad_branch[...], flat(m.w_out, 0, width), 1, 1).astype(BF16)
+
+    def back_score(self, i):
         m, width = self.m, self.width
         ones = head_ones()
-        scale = HEAD**-0.5
 
         def score(p, carry):
             product = m.attended[...].astype(F32) * m.key_value[p, :, width:].astype(F32)
             m.grad_prob[p] = head_sum(product, ones)
             return carry
 
-        lax.fori_loop(0, PIECES, score, 0)
+        lax.fori_loop(*self.half_of(PIECES, i), score, 0)
+
+    def back_soft(self, half):
+        m, width = self.m, self.width
+        scale = HEAD**-0.5
 
         def soft(i, carry):
             span = pl.ds(pl.multiple_of(i * 16, 16), 16)
@@ -603,28 +618,24 @@
             m.query[span, :] = (grad_query * scale).astype(BF16)
             return carry
 
-        lax.fori_loop(0, self.total // 16, soft, 0)
-
-    def qkv_back(self):
+        lax.fori_loop(*self.half_of(self.total // 16, half), soft, 0)
+
+    def qkv_back(self, i):
         m, width = self.m, self.width
-        lead = m.d_qkv.shape[:-1]
-        step = 2 * LANES
-        m.d_qkv[:, :, :, :, :, :width] = (
-            contract(m.normed[0], m.query[...], 0, 0).astype(BF16).reshape(lead + (width,))
+        if i == 4:
+            self.put(m.d_q, contract(m.normed[0], m.query[...], 0, 0))
+            return
+        step = width // 2
+        grad = contract(
+            m.normed[...].reshape(PIECES * self.total, width),
+            m.key_value[:, :, i * step : (i + 1) * step].reshape(PIECES * self.total, step),
+            0,
+            0,
         )
-
-        def one(j, carry):
-            target = pl.ds(pl.multiple_of(width + j * step, step), step)
-            span = pl.ds(pl.multiple_of(j * step, step), step)
-            grad = m.key_value[:, :, span].reshape(PIECES * self.total, step)
-            m.d_qkv[:, :, :, :, :, target] = (
-                contract(m.normed[...].reshape(PIECES * self.total, width), grad, 0, 0)
-                .astype(BF16)
-                .reshape(lead + (step,))
-            )
-            return carry
-
-        lax.fori_loop(0, 2 * width // step, one, 0)
+        target, low = (m.d_k, m.d_v)[i // 2], (i % 2) * step
+        target[:, :, :, :, :, low : low + step] = grad.astype(BF16).reshape(
+            target.shape[:-1] + (step,)
+        )
 
     def normed_back(self):
         m, width = self.m, self.width
@@ -661,11 +672,11 @@
 
         for p in range(PIECES):
             back(p)
-        lead = m.d_qkv.shape[:-1]
+        lead = m.d_out.shape[:-1]
         small = jnp.concatenate(
             [m.d_small[...], jnp.zeros((LANES - 8, width), F32)], axis=0
         ).T
-        m.d_qkv[:, :, :, :, :, 3 * width :] = small.astype(BF16).reshape(lead + (LANES,))
+        m.d_out[:, :, :, :, :, width:] = small.astype(BF16).reshape(lead + (LANES,))
 
 
 def block_scratch(n, rows, total, width, hidden, out_width):
@@ -695,28 +706,74 @@
     )
 
 
-NAMES = ("qkv", "out", "up", "down", "proj")
+NAMES = ("out", "qkv", "up", "down", "proj")
+
+
+SHARES = 18
+SUMS = dict(
+    proj0=("proj", 0),
+    proj1=("proj", 1),
+    down0=("down", 0),
+    down1=("down", 1),
+    up0=("up", 0),
+    up1=("up", 1),
+    k=("qkv", 1),
+    v=("qkv", 2),
+    q=("qkv", 0),
+    out=("out", 0),
+)
 
 
 def main_kernel(n_entries, names, segs, seg_rows, rows, *refs):
     m = types.SimpleNamespace(**dict(zip(names, refs)))
     place = Place(n_entries)
     n, half = place.n, place.n // 2
+    peers = partners(place)
+    barrier = pltpu.get_barrier_semaphore()
+    for peer in peers:
+        pl.semaphore_signal(barrier, inc=1, device_id=peer, device_id_type=MESH)
     shard = m.ln1_gain.shape[0]
+    width = m.i_pieces.shape[2]
+    mine = {
+        name: getattr(m, "w_" + name).at[place.z, place.x, place.c, place.y] for name in NAMES
+    }
+    targets = dict(
+        i_ln1_gain=m.ln1_gain,
+        i_ln2_gain=m.ln2_gain,
+        i_group_table=m.group_table,
+        i_out=mine["out"].at[:, :width],
+        i_qkv=mine["qkv"],
+        i_up=mine["up"],
+        i_down=mine["down"],
+        i_proj=mine["proj"],
+        i_text_ids=m.text_ids,
+        i_text_mask=m.text_mask,
+        i_lengths=m.lengths,
+        i_groups=m.groups,
+        i_pieces=m.pieces,
+        i_grad_embed=m.grad_embed,
+    )
+    inward = [
+        pltpu.make_async_copy(getattr(m, name), target, m.i_sem.at[i])
+        for i, (name, target) in enumerate(targets.items())
+    ]
+    for copy in inward:
+        copy.start()
     m.n_groups = m.group_table.shape[0]
     feats = m.grad_embed.shape[0]
     block = Block(m, segs, seg_rows, rows, feats)
-    width = block.width
     gather, reduce = types.SimpleNamespace(), types.SimpleNamespace()
     for i, name in enumerate(NAMES):
-        whole, parts = getattr(m, "w_" + name), getattr(m, "d_" + name)
+        whole = getattr(m, "w_" + name)
         setattr(gather, name, Gather(place, whole, m.g_send.at[i], m.g_recv.at[i]))
-        held = [getattr(m, f"{kind}_{name}") for kind in ("core", "one", "two", "along")]
-        setattr(reduce, name, Reduce(place, parts, *held, m.r_send.at[i], m.r_recv.at[i]))
-        if name != "qkv":
-            whole[place.z, place.x, place.c, place.y] = getattr(m, "s_" + name)[...]
-    mine = m.w_qkv.at[place.z, place.x, place.c, place.y]
-    mine[:, : 3 * width] = m.s_qkv[...]
+    for i, name in enumerate(SUMS):
+        held = [getattr(m, f"{kind}_{name}") for kind in ("d", "core", "one", "two", "along")]
+        part = Reduce(place, *held, m.r_send.at[i], m.r_recv.at[i])
+        part.stage, part.place_in = getattr(m, "t_" + name), SUMS[name][1]
+        part.target = getattr(m, "o_" + SUMS[name][0])
+        setattr(reduce, name, part)
+    for copy in inward[:3]:
+        copy.wait()
     small = jnp.concatenate(
         [
             m.ln1_gain[...].astype(F32).reshape(1, shard),
@@ -728,44 +785,44 @@
     )
     small = jnp.concatenate([small, jnp.zeros((8, LANES - shard), F32)], axis=1).T
     small = jnp.concatenate([small[:shard], jnp.zeros((shard, LANES - 8), F32)], axis=1)
-    mine[:, 3 * width :] = small.astype(BF16)
-    meet(place)
-    gather.out.z_start()
-    gather.qkv.z_start()
-
+    mine["out"][:, width:] = small.astype(BF16)
+    for copy in inward[3:8]:
+        copy.wait()
     text_len = m.text_ids.shape[0]
-    text_keys(
-        block.number, seg_rows, rows, segs, half, m.text_ids, m.text_mask, m.row_key, m.seg_key
-    )
     acc = m.grad_prob.reshape(PIECES * block.total, width)
     acc = acc.at[pl.ds(0, half * rows // 2), pl.ds(0, 4 * LANES)]
-    acc[...] = jnp.zeros(acc.shape, F32)
     scatter = Sweep(
         text_len,
         lambda start, count: scatter_block(
             start, count, m.row_key, m.seg_key, m.grad_embed, acc
         ),
     )
-    scatter.go(2)
-    gather.out.z_wait()
-    gather.up.z_start()
-    scatter.go(3)
-    gather.qkv.z_wait()
-    block.load()
-    gather.out.one_wait()
-    gather.out.two_wait()
-    scatter.go(3)
-    gather.out.three_wait()
-    gather.qkv.one_wait()
-    gather.down.z_start()
-    scatter.go(3)
-    gather.qkv.two_wait()
-    gather.up.z_wait()
-    gather.proj.z_start()
-    scatter.go(3)
-    gather.qkv.three_wait()
-    gather.out.core_wait()
-    scatter.go()
+    lookup = Sweep(
+        text_len,
+        lambda start, count: lookup_block(
+            start, count, m.row_key, m.seg_key, m.table, m.found
+        ),
+    )
+    grad_way = (place, m.sent_grad, m.came_grad, m.xg_send, m.xg_recv)
+    table_way = (place, m.came_grad, m.came_table, m.xt_send, m.xt_recv)
+    going = []
+
+    def send_out(source, target):
+        going.append(pltpu.make_async_copy(source, target, m.o_sem.at[len(going)]))
+        going[-1].start()
+
+    def keys():
+        for copy in inward[8:10]:
+            copy.wait()
+        text_keys(
+            block.number, seg_rows, rows, segs, half, m.text_ids, m.text_mask, m.row_key, m.seg_key
+        )
+        acc[...] = jnp.zeros(acc.shape, F32)
+
+    def load():
+        for copy in inward[10:]:
+            copy.wait()
+        block.load()
 
     def pack(i, carry):
         span = pl.ds(pl.multiple_of(i * rows, rows), rows)
@@ -774,113 +831,234 @@
             m.sent_grad[i + (k // 2) * (half // 2) + (k % 2) * half] = value.astype(BF16)
         return carry
 
-    lax.fori_loop(0, half // 2, pack, 0)
+    def scatter_end():
+        lax.fori_loop(0, half // 2, pack, 0)
+
+    def norm_back():
+        block.norm_back()
+        send_out(m.grad_pieces, m.o_pieces)
+
+    def look_prep():
+        for side in range(2):
+            part = m.came_table[side * half : (side + 1) * half].reshape(half * rows, LANES)
+            m.table[side * LANES : (side + 1) * LANES, :] = part.astype(F32).T.astype(BF16)
+
+    def result(part):
+        stage = part.stage
+        part.z_wait(stage)
+        if part is reduce.out:
+            small = jnp.concatenate(
+                [stage[:, width:], jnp.zeros((LANES - shard, LANES), F32)], axis=0
+            ).T
+            m.t_ln1[...] = small[0:1, :shard].reshape(shard)
+            m.t_ln2[...] = small[1:2, :shard].reshape(shard)
+            m.t_group[...] = small[2 : 2 + m.n_groups, :shard]
+            send_out(m.t_ln1, m.o_ln1)
+            send_out(m.t_ln2, m.o_ln2)
+            send_out(m.t_group, m.o_group)
+            send_out(stage.at[:, :width], m.o_out)
+        else:
+            columns = stage.shape[1]
+            low = part.place_in * columns
+            send_out(stage, part.target.at[:, low : low + columns])
+
+    def sent_all():
+        exchange_wait(*grad_way, True)
+        for name in NAMES:
+            getattr(gather, name).finish()
+
+    pl.semaphore_wait(barrier, len(peers))
+    gather.out.start()
+    gather.qkv.start()
+    gather.up.start()
+    keys()
+    load()
+    scatter.go(0, 5)
+    gather.out.one_wait(0)
+    gather.out.z_wait(0)
+    scatter.go(5, 6)
+    gather.out.z_wait(1)
+    gather.qkv.one_wait(0)
+    gather.out.z_wait(2)
+    gather.down.start()
+    scatter.go(6, 8)
+    gather.qkv.z_wait(0)
+    gather.up.one_wait(0)
+    scatter.go(8, 10)
+    gather.out.one_wait(1)
+    scatter.go(10, 11)
+    gather.out.one_wait(2)
+    gather.qkv.z_wait(1)
+    gather.out.one_wait(3)
+    scatter.go(11, 13)
+    gather.qkv.z_wait(2)
+    gather.out.two_wait()
+    gather.down.one_wait(0)
+    scatter.go(13, 15)
+    gather.up.z_wait(0)
+    gather.qkv.one_wait(1)
+    scatter.go(15, 17)
+    gather.qkv.one_wait(2)
+    scatter.go(17, 18)
+    scatter_end()
+    gather.qkv.one_wait(3)
+    gather.up.z_wait(1)
+    gather.out.three_wait()
+    gather.up.z_wait(2)
+    gather.up.one_wait(1)
+    gather.qkv.two_wait()
+    gather.out.core_wait()
+    gather.down.z_wait(0)
+    exchange(*grad_way)
+    gather.proj.start()
+    gather.up.one_wait(2)
+    gather.up.one_wait(3)
+    gather.down.z_wait(1)
+    gather.down.one_wait(1)
+    gather.down.z_wait(2)
+    gather.qkv.three_wait()
     gather.qkv.core_wait()
     block.norm_one()
-    gather.up.one_wait()
     gather.up.two_wait()
-    block.project_qkv()
-    gather.down.z_wait()
-    exchange(place, m.sent_grad, m.came_grad, m.xg_send, m.xg_recv)
+    block.project_qkv(0)
+    block.project_qkv(1)
+    block.project_qkv(2)
+    block.project_qkv(3)
+    block.project_qkv(4)
+    block.score(0)
+    block.score(1)
+    gather.proj.one_wait(0)
+    block.soft(0)
+    gather.down.one_wait(2)
+    block.soft(1)
+    block.norm_two()
+    gather.down.one_wait(3)
+    exchange_wait(*grad_way, False)
+    block.table_back(0)
     gather.up.three_wait()
-    block.attend()
-    block.norm_two()
-    gather.down.one_wait()
+    block.table_back(1)
+    gather.proj.z_wait(0)
     gather.down.two_wait()
     gather.up.core_wait()
-    block.up()
-    gather.proj.z_wait()
+    block.up(0)
+    block.up(1)
+    block.up(2)
+    gather.proj.z_wait(1)
+    block.up(3)
     gather.down.three_wait()
-    gather.proj.one_wait()
-    gather.proj.two_wait()
+    gather.proj.z_wait(2)
+    gather.proj.one_wait(1)
     gather.down.core_wait()
     block.down()
-    exchange_wait(place, m.sent_grad, m.came_grad, m.xg_send, m.xg_recv, False)
-    block.table_back()
-    block.proj_grad()
-    reduce.proj.core_start()
+    block.proj_grad(0)
+    reduce.proj0.core_start()
+    block.proj_grad(1)
+    reduce.proj1.core_start()
+    gather.proj.one_wait(2)
+    reduce.proj0.core_wait()
+    gather.proj.one_wait(3)
+    gather.proj.two_wait()
+    reduce.proj1.core_wait()
     gather.proj.three_wait()
-    reduce.proj.core_wait()
+    reduce.proj0.one_wait()
     gather.proj.core_wait()
+    reduce.proj0.one_more_wait()
+    block.table(0)
+    block.table(1)
+    block.table(2)
+    block.table(3)
+    exchange(*table_way)
+    reduce.proj1.one_wait()
     block.proj_back()
-    block.down_grad()
-    reduce.down.core_start()
-    block.table()
-    exchange(place, m.came_grad, m.came_table, m.xt_send, m.xt_recv)
+    block.down_grad(0)
+    reduce.down0.core_start()
+    block.down_grad(1)
+    reduce.down1.core_start()
+    reduce.proj0.two_wait()
     block.down_back()
-    block.up_grad()
-    reduce.up.core_start()
-    reduce.down.core_wait()
+    reduce.proj1.one_more_wait()
+    reduce.down0.core_wait()
+    block.up_grad(0)
+    reduce.up0.core_start()
+    block.up_grad(1)
+    reduce.up1.core_start()
     block.up_back()
+    reduce.down1.core_wait()
     block.out_back()
+    block.back_score(0)
+    block.back_score(1)
+    block.back_soft(0)
+    block.back_soft(1)
+    block.qkv_back(0)
+    reduce.up0.core_wait()
+    block.qkv_back(1)
+    reduce.k.core_start()
+    block.qkv_back(2)
+    reduce.proj1.two_wait()
+    reduce.down0.one_wait()
+    reduce.up1.core_wait()
+    block.qkv_back(3)
+    reduce.v.core_start()
+    reduce.down0.one_more_wait()
+    block.qkv_back(4)
+    reduce.q.core_start()
+    block.normed_back()
+    reduce.down1.one_wait()
+    exchange_wait(*table_way, False)
+    norm_back()
     reduce.out.core_start()
-    reduce.proj.one_wait()
-    block.attend_back()
-    reduce.up.core_wait()
-    block.qkv_back()
-    reduce.proj.two_wait()
-    block.normed_back()
-    reduce.down.one_wait()
-    block.norm_back()
-    reduce.qkv.core_start()
-    pieces_out = pltpu.make_async_copy(m.grad_pieces, m.o_pieces, m.o_sem.at[0])
-    pieces_out.start()
-    reduce.qkv.core_wait()
-    reduce.down.two_wait()
-    exchange_wait(place, m.came_grad, m.came_table, m.xt_send, m.xt_recv, False)
-    for side in range(2):
-        part = m.came_table[side * half : (side + 1) * half].reshape(half * rows, LANES)
-        m.table[side * LANES : (side + 1) * LANES, :] = part.astype(F32).T.astype(BF16)
-    lookup = Sweep(
-        text_len,
-        lambda start, count: lookup_block(
-            start, count, m.row_key, m.seg_key, m.table, m.found
-        ),
-    )
-    outs = []
-
-    def finish(i, name):
-        stage = getattr(m, "t_" + name)
-        getattr(reduce, name).z_wait(stage)
-        source = stage.at[:, : 3 * width] if name == "qkv" else stage
-        outs.append(pltpu.make_async_copy(source, getattr(m, "o_" + name), m.o_sem.at[i]))
-        outs[-1].start()
-
-    lookup.go(3)
-    reduce.up.one_wait()
-    lookup.go(2)
-    finish(1, "proj")
-    lookup.go(2)
+    reduce.down1.one_more_wait()
+    reduce.k.core_wait()
+    reduce.down0.two_wait()
+    look_prep()
+    result(reduce.proj0)
+    lookup.go(0, 2)
+    reduce.up0.one_wait()
+    reduce.v.core_wait()
+    lookup.go(2, 4)
+    reduce.down1.two_wait()
+    result(reduce.proj1)
+    lookup.go(4, 5)
+    reduce.up0.one_more_wait()
+    reduce.q.core_wait()
+    lookup.go(5, 8)
     reduce.out.core_wait()
-    reduce.up.two_wait()
-    lookup.go(2)
-    reduce.qkv.one_wait()
-    lookup.go(2)
-    finish(2, "down")
-    lookup.go(2)
-    reduce.qkv.two_wait()
-    lookup.go(2)
+    reduce.up1.one_wait()
+    result(reduce.down0)
+    lookup.go(8, 10)
+    reduce.up0.two_wait()
+    lookup.go(10, 11)
+    reduce.up1.one_more_wait()
+    lookup.go(11, 12)
+    reduce.k.one_wait()
+    result(reduce.down1)
+    lookup.go(12, 14)
+    reduce.k.one_more_wait()
+    lookup.go(14, 16)
+    reduce.v.one_wait()
+    reduce.up1.two_wait()
+    sent_all()
+    lookup.go(16, 18)
+    send_out(m.found, m.o_found)
+    reduce.k.two_wait()
+    reduce.v.one_more_wait()
+    result(reduce.up0)
+    reduce.q.one_wait()
+    reduce.q.one_more_wait()
+    reduce.v.two_wait()
     reduce.out.one_wait()
-    finish(3, "up")
-    lookup.go()
-    found_out = pltpu.make_async_copy(m.found, m.o_found, m.o_sem.at[4])
-    found_out.start()
+    result(reduce.up1)
+    reduce.out.one_more_wait()
+    reduce.q.two_wait()
+    result(reduce.k)
     reduce.out.two_wait()
-    finish(5, "qkv")
-    small = m.t_qkv[:, 3 * width :]
-    small = jnp.concatenate([small, jnp.zeros((LANES - shard, LANES), F32)], axis=0).T
-    m.o_ln1[...] = small[0:1, :shard].reshape(shard)
-    m.o_ln2[...] = small[1:2, :shard].reshape(shard)
-    m.o_group[...] = small[2 : 2 + m.n_groups, :shard]
-    finish(6, "out")
-    exchange_wait(place, m.sent_grad, m.came_grad, m.xg_send, m.xg_recv, True)
-    exchange_wait(place, m.came_grad, m.came_table, m.xt_send, m.xt_recv, True)
-    for name in NAMES:
-        getattr(gather, name).finish()
+    result(reduce.v)
+    result(reduce.q)
+    result(reduce.out)
+    exchange_wait(*table_way, True)
+    for name in SUMS:
         getattr(reduce, name).finish()
-    pieces_out.wait()
-    found_out.wait()
-    for copy in outs:
+    for copy in going:
         copy.wait()
 
 
@@ -930,25 +1108,24 @@
     rows = -(-seg_rows // 16) * 16
     half, total = n // 2, segs * rows
     pieces = jnp.transpose(pieces, (1, 0, 2))
-    vmem = pl.BlockSpec(memory_space=VMEM)
     hbm = pl.BlockSpec(memory_space=pl.ANY)
     dma = pltpu.SemaphoreType.DMA
 
     ins = dict(
-        pieces=pieces,
-        lengths=lengths,
-        groups=entry_group,
-        group_table=group_table,
-        ln1_gain=ln1_gain,
-        s_qkv=w_qkv,
-        s_out=w_out,
-        ln2_gain=ln2_gain,
-        s_up=w_up,
-        s_down=w_down,
-        s_proj=w_proj,
-        text_ids=text_ids,
-        text_mask=text_mask,
-        grad_embed=grad_embed,
+        i_pieces=pieces,
+        i_lengths=lengths,
+        i_groups=entry_group,
+        i_group_table=group_table,
+        i_ln1_gain=ln1_gain,
+        i_qkv=w_qkv,
+        i_out=w_out,
+        i_ln2_gain=ln2_gain,
+        i_up=w_up,
+        i_down=w_down,
+        i_proj=w_proj,
+        i_text_ids=text_ids,
+        i_text_mask=text_mask,
+        i_grad_embed=grad_embed,
     )
     outs = dict(
         o_found=full((feats, text_len), BF16),
@@ -962,7 +1139,6 @@
         o_down=full(w_down.shape, F32),
         o_proj=full(w_proj.shape, F32),
     )
-    tiny = ("o_group", "o_ln1", "o_ln2")
     scratch = {
         name: VMEM(*item)
         for name, item in block_scratch(
@@ -971,14 +1147,18 @@
     }
     lead = (n_z, 2, 2, 2)
     shapes = dict(
-        qkv=(w_qkv.shape[0], w_qkv.shape[1] + LANES),
-        out=w_out.shape,
+        out=(w_out.shape[0], width + LANES),
+        qkv=w_qkv.shape,
         up=w_up.shape,
         down=w_down.shape,
         proj=w_proj.shape,
     )
     for name, shape in shapes.items():
         scratch["w_" + name] = VMEM(lead + shape, BF16)
+    for name, (whole, _) in SUMS.items():
+        shape = shapes[whole]
+        parts_n = 3 if whole == "qkv" else 1 if whole == "out" else 2
+        shape = (shape[0], shape[1] // parts_n)
         scratch["d_" + name] = VMEM(lead + shape, BF16)
         scratch["t_" + name] = VMEM(shape, F32)
         scratch["core_" + name] = VMEM((n_z, 2, 2) + shape, BF16)
@@ -993,16 +1173,24 @@
         table=VMEM((2 * LANES, half * rows), BF16),
         found=VMEM((feats, text_len), BF16),
         grad_pieces=VMEM(pieces.shape, BF16),
-        g_send=dma((len(NAMES), n_z + 6)),
-        g_recv=dma((len(NAMES), n_z + 6)),
-        r_send=dma((len(NAMES), n_z + 4)),
-        r_recv=dma((len(NAMES), n_z + 4)),
-        xg_send=dma((n,)),
-        xg_recv=dma((n,)),
-        xt_send=dma((n,)),
-        xt_recv=dma((n,)),
-        o_sem=dma((7,)),
-    )
+        i_sem=dma((len(ins),)),
+        t_ln1=VMEM(ln1_gain.shape, F32),
+        t_ln2=VMEM(ln2_gain.shape, F32),
+        t_group=VMEM(group_table.shape, F32),
+        g_send=dma((len(NAMES),)),
+        g_recv=dma((len(NAMES), 2 * n_z + 2)),
+        r_send=dma((len(SUMS),)),
+        r_recv=dma((len(SUMS), 5)),
+        xg_send=dma(()),
+        xg_recv=dma(()),
+        xt_send=dma(()),
+        xt_recv=dma(()),
+        o_sem=dma((len(SUMS) + 5,)),
+    )
+    for name in ("pieces", "lengths", "groups", "group_table", "ln1_gain", "ln2_gain"):
+        scratch[name] = VMEM(ins["i_" + name].shape, ins["i_" + name].dtype)
+    for name in ("text_ids", "text_mask", "grad_embed"):
+        scratch[name] = VMEM(ins["i_" + name].shape, ins["i_" + name].dtype)
     results = pl.pallas_call(
         functools.partial(
             main_kernel,
@@ -1013,8 +1201,8 @@
             rows,
         ),
         out_shape=tuple(outs.values()),
-        in_specs=[vmem] * len(ins),
-        out_specs=tuple(vmem if name in tiny else hbm for name in outs),
+        in_specs=[hbm] * len(ins),
+        out_specs=(hbm,) * len(outs),
         scratch_shapes=list(scratch.values()),
         compiler_params=pltpu.CompilerParams(
             collective_id=0, has_side_effects=True, vmem_limit_bytes=VMEM_BYTES

time: 131 us -> 106 us (0.81)
  Pallas kernels: 130 us -> 105 us
    pallas_call x1, Pallas kernels: 127 us -> 102 us  [body(): pl.pallas_call(functools.partial(main_kernel, n_entries, tuple(ins) + tup...]
where the time goes in v2:
time: 106 us
  Pallas kernels  105 us (99%)
    pallas_call x1, Pallas kernels, body(): pl.pallas_call(functools.partial(main_kernel, n_entries, tuple(ins) + tup...  102 us
    pallas_call x1, Pallas kernels, body(): pl.pallas_call(functools.partial(copy_kernel, len(results)), out_shape=tu...  3.01 us

profile of v2, /device:TPU:0, one launch (start us, length us, event | category | flops | bytes accessed | tf_op | source)
XLA Modules:
  0.0 106.1 jit_solution(9889467430788179728)
XLA Ops:
  0.6 102.3 %shard_map.213 = (bf16[64,9344]{1,0:T(8,128)(2,1)}, bf16[7,146,512]{2,1,0:T(8,128)(2,1)}, f32[4,16]{1,0:T(4,128)}, f32[16]{0:T(128)}, f32[16,1536]{1,0:T(8,128)}...) custom-call(bf16[7,146,512]{2,1,0:T(8,128)(2,1)} %bitcast.2, ...), custom_call_target="tpu_custom_call" | custom-call | tf_op jit(solution)/shard_map/pallas_call | solution.py:1194
  102.9 3.0 %shard_map.214 = (bf16[64,9344]{1,0:T(8,128)(2,1)}, bf16[7,146,512]{2,1,0:T(8,128)(2,1)}, f32[4,16]{1,0:T(4,128)}, f32[16]{0:T(128)}, f32[16,1536]{1,0:T(8,128)}...) custom-call(bf16[64,9344]{1,0:T(8,128)(2,1)} %get-tuple-element.30.refs_0_,, ...), custom_call_target="tpu_custom_call" | custom-call | tf_op jit(solution)/shard_map/pallas_call | solution.py:1211

commit v3 on v2

--- a/solution.py
+++ b/solution.py
@@ -75,7 +75,7 @@
 
 
 class Gather:
-    def __init__(self, place, whole, send, recv):
+    def __init__(self, place, whole, send, recv, source=None):
         p = self.place = place
         nz = p.n_z
         self.groups = thirds(nz)
@@ -89,13 +89,18 @@
         def copy(ref, index, to):
             return remote(ref, ref, send, recv.at[index], to)
 
+        def first(index, to):
+            ref = shard(0, p.x, p.y)
+            return remote(ref if source is None else source, ref, send, recv.at[index], to)
+
         self.along = {
-            k: copy(shard(0, p.x, p.y), k - 1, p.at(p.along_z(k), p.x, p.c, p.y))
-            for k in range(1, nz)
+            k: first(k - 1, p.at(p.along_z(k), p.x, p.c, p.y)) for k in range(1, nz)
         }
         self.one = [copy(shard(k, p.x, p.y), nz - 1 + k, to_one) for k in range(nz)]
+        self.one[0] = first(nz - 1, to_one)
         base = 2 * nz - 1
         self.two = [copy(shard(k, p.x, p.y), base, to_two) for k in range(nz)]
+        self.two[0] = first(base, to_two)
         self.three = [copy(shard(k, p.x1, p.y1), base + 1, to_two) for k in range(nz)]
         cols = [(p.x, p.y), (p.x1, p.y1), (p.x2, p.y2), (1 - p.x, 1 - p.y)]
         self.core = [copy(whole.at[:, x, p.c, y], base + 2, to_core) for x, y in cols]
@@ -227,7 +232,8 @@
     dst[place.line] = src[place.line]
 
     def begin(step, carry):
-        other = lax.rem(place.line + step, place.n)
+        turn = lax.rem(step + 3 * place.n // 4 - 1, place.n - 1) + 1
+        other = lax.rem(place.line + turn, place.n)
         to = (lax.div(other, 2), lax.rem(other, 2))
         remote(src.at[other], dst.at[place.line], send, recv, to).start()
         return carry
@@ -742,12 +748,12 @@
         i_ln2_gain=m.ln2_gain,
         i_group_table=m.group_table,
         i_out=mine["out"].at[:, :width],
+        i_text_ids=m.text_ids,
+        i_text_mask=m.text_mask,
         i_qkv=mine["qkv"],
         i_up=mine["up"],
         i_down=mine["down"],
         i_proj=mine["proj"],
-        i_text_ids=m.text_ids,
-        i_text_mask=m.text_mask,
         i_lengths=m.lengths,
         i_groups=m.groups,
         i_pieces=m.pieces,
@@ -765,7 +771,8 @@
     gather, reduce = types.SimpleNamespace(), types.SimpleNamespace()
     for i, name in enumerate(NAMES):
         whole = getattr(m, "w_" + name)
-        setattr(gather, name, Gather(place, whole, m.g_send.at[i], m.g_recv.at[i]))
+        source = None if name == "out" else getattr(m, "i_" + name)
+        setattr(gather, name, Gather(place, whole, m.g_send.at[i], m.g_recv.at[i], source))
     for i, name in enumerate(SUMS):
         held = [getattr(m, f"{kind}_{name}") for kind in ("d", "core", "one", "two", "along")]
         part = Reduce(place, *held, m.r_send.at[i], m.r_recv.at[i])
@@ -786,8 +793,7 @@
     small = jnp.concatenate([small, jnp.zeros((8, LANES - shard), F32)], axis=1).T
     small = jnp.concatenate([small[:shard], jnp.zeros((shard, LANES - 8), F32)], axis=1)
     mine["out"][:, width:] = small.astype(BF16)
-    for copy in inward[3:8]:
-        copy.wait()
+    inward[3].wait()
     text_len = m.text_ids.shape[0]
     acc = m.grad_prob.reshape(PIECES * block.total, width)
     acc = acc.at[pl.ds(0, half * rows // 2), pl.ds(0, 4 * LANES)]
@@ -812,7 +818,7 @@
         going[-1].start()
 
     def keys():
-        for copy in inward[8:10]:
+        for copy in inward[4:10]:
             copy.wait()
         text_keys(
             block.number, seg_rows, rows, segs, half, m.text_ids, m.text_mask, m.row_key, m.seg_key
@@ -870,7 +876,6 @@
     pl.semaphore_wait(barrier, len(peers))
     gather.out.start()
     gather.qkv.start()
-    gather.up.start()
     keys()
     load()
     scatter.go(0, 5)
@@ -880,10 +885,9 @@
     gather.out.z_wait(1)
     gather.qkv.one_wait(0)
     gather.out.z_wait(2)
-    gather.down.start()
+    gather.up.start()
     scatter.go(6, 8)
     gather.qkv.z_wait(0)
-    gather.up.one_wait(0)
     scatter.go(8, 10)
     gather.out.one_wait(1)
     scatter.go(10, 11)
@@ -892,8 +896,9 @@
     gather.out.one_wait(3)
     scatter.go(11, 13)
     gather.qkv.z_wait(2)
+    gather.down.start()
     gather.out.two_wait()
-    gather.down.one_wait(0)
+    gather.up.one_wait(0)
     scatter.go(13, 15)
     gather.up.z_wait(0)
     gather.qkv.one_wait(1)
@@ -904,145 +909,149 @@
     gather.qkv.one_wait(3)
     gather.up.z_wait(1)
     gather.out.three_wait()
+    gather.down.one_wait(0)
     gather.up.z_wait(2)
-    gather.up.one_wait(1)
     gather.qkv.two_wait()
     gather.out.core_wait()
-    gather.down.z_wait(0)
     exchange(*grad_way)
     gather.proj.start()
+    gather.up.one_wait(1)
+    gather.down.z_wait(0)
     gather.up.one_wait(2)
     gather.up.one_wait(3)
     gather.down.z_wait(1)
-    gather.down.one_wait(1)
     gather.down.z_wait(2)
     gather.qkv.three_wait()
     gather.qkv.core_wait()
     block.norm_one()
-    gather.up.two_wait()
     block.project_qkv(0)
     block.project_qkv(1)
+    gather.up.two_wait()
+    gather.proj.one_wait(0)
     block.project_qkv(2)
     block.project_qkv(3)
+    gather.down.one_wait(1)
     block.project_qkv(4)
     block.score(0)
+    gather.down.one_wait(2)
     block.score(1)
-    gather.proj.one_wait(0)
     block.soft(0)
-    gather.down.one_wait(2)
+    gather.down.one_wait(3)
     block.soft(1)
     block.norm_two()
-    gather.down.one_wait(3)
     exchange_wait(*grad_way, False)
     block.table_back(0)
-    gather.up.three_wait()
     block.table_back(1)
     gather.proj.z_wait(0)
+    gather.up.three_wait()
     gather.down.two_wait()
     gather.up.core_wait()
     block.up(0)
     block.up(1)
+    gather.proj.z_wait(1)
     block.up(2)
-    gather.proj.z_wait(1)
     block.up(3)
-    gather.down.three_wait()
     gather.proj.z_wait(2)
     gather.proj.one_wait(1)
+    gather.down.three_wait()
     gather.down.core_wait()
     block.down()
+    gather.proj.one_wait(2)
     block.proj_grad(0)
     reduce.proj0.core_start()
     block.proj_grad(1)
     reduce.proj1.core_start()
-    gather.proj.one_wait(2)
-    reduce.proj0.core_wait()
     gather.proj.one_wait(3)
     gather.proj.two_wait()
+    reduce.proj0.core_wait()
     reduce.proj1.core_wait()
     gather.proj.three_wait()
+    gather.proj.core_wait()
+    block.table(0)
     reduce.proj0.one_wait()
-    gather.proj.core_wait()
-    reduce.proj0.one_more_wait()
-    block.table(0)
     block.table(1)
     block.table(2)
     block.table(3)
     exchange(*table_way)
+    reduce.proj0.one_more_wait()
+    block.proj_back()
     reduce.proj1.one_wait()
-    block.proj_back()
     block.down_grad(0)
     reduce.down0.core_start()
     block.down_grad(1)
     reduce.down1.core_start()
-    reduce.proj0.two_wait()
     block.down_back()
-    reduce.proj1.one_more_wait()
-    reduce.down0.core_wait()
     block.up_grad(0)
     reduce.up0.core_start()
+    reduce.down0.core_wait()
+    reduce.proj0.two_wait()
+    reduce.proj1.one_more_wait()
     block.up_grad(1)
     reduce.up1.core_start()
     block.up_back()
+    block.out_back()
     reduce.down1.core_wait()
-    block.out_back()
     block.back_score(0)
     block.back_score(1)
     block.back_soft(0)
     block.back_soft(1)
     block.qkv_back(0)
-    reduce.up0.core_wait()
     block.qkv_back(1)
     reduce.k.core_start()
+    reduce.up0.core_wait()
     block.qkv_back(2)
-    reduce.proj1.two_wait()
-    reduce.down0.one_wait()
-    reduce.up1.core_wait()
     block.qkv_back(3)
     reduce.v.core_start()
-    reduce.down0.one_more_wait()
     block.qkv_back(4)
     reduce.q.core_start()
+    reduce.down0.one_wait()
+    reduce.proj1.two_wait()
     block.normed_back()
-    reduce.down1.one_wait()
+    reduce.down0.one_more_wait()
     exchange_wait(*table_way, False)
+    reduce.up1.core_wait()
     norm_back()
     reduce.out.core_start()
-    reduce.down1.one_more_wait()
+    reduce.down1.one_wait()
+    look_prep()
+    lookup.go(0, 1)
+    result(reduce.proj0)
     reduce.k.core_wait()
     reduce.down0.two_wait()
-    look_prep()
-    result(reduce.proj0)
-    lookup.go(0, 2)
+    reduce.down1.one_more_wait()
+    lookup.go(1, 4)
     reduce.up0.one_wait()
     reduce.v.core_wait()
-    lookup.go(2, 4)
+    result(reduce.proj1)
+    lookup.go(4, 7)
     reduce.down1.two_wait()
-    result(reduce.proj1)
-    lookup.go(4, 5)
+    lookup.go(7, 8)
     reduce.up0.one_more_wait()
     reduce.q.core_wait()
-    lookup.go(5, 8)
+    lookup.go(8, 9)
+    result(reduce.down0)
+    lookup.go(9, 10)
     reduce.out.core_wait()
+    lookup.go(10, 11)
     reduce.up1.one_wait()
-    result(reduce.down0)
-    lookup.go(8, 10)
+    lookup.go(11, 12)
     reduce.up0.two_wait()
-    lookup.go(10, 11)
+    lookup.go(12, 13)
     reduce.up1.one_more_wait()
-    lookup.go(11, 12)
+    lookup.go(13, 14)
     reduce.k.one_wait()
+    lookup.go(14, 15)
     result(reduce.down1)
-    lookup.go(12, 14)
+    lookup.go(15, 16)
     reduce.k.one_more_wait()
-    lookup.go(14, 16)
-    reduce.v.one_wait()
-    reduce.up1.two_wait()
     sent_all()
     lookup.go(16, 18)
+    reduce.v.one_wait()
     send_out(m.found, m.o_found)
-    reduce.k.two_wait()
+    reduce.up1.two_wait()
     reduce.v.one_more_wait()
     result(reduce.up0)
+    reduce.k.two_wait()
     reduce.q.one_wait()
     reduce.q.one_more_wait()
     reduce.v.two_wait()
@@ -1062,18 +1071,36 @@
         copy.wait()
 
 
+def pieces_of_result(ref):
+    if ref.shape[0] * ref.shape[-1] < 2**18 and len(ref.shape) < 3:
+        return [ref]
+    if len(ref.shape) == 3:
+        return [ref.at[pl.ds(k, 1)] for k in range(ref.shape[0])]
+    steps = max(ref.shape[0] // 16, 1)
+    size = ref.shape[0] // steps
+    return [ref.at[pl.ds(k * size, size)] for k in range(steps)]
+
+
 def copy_kernel(count, *refs):
     ins, outs, held = refs[:count], refs[count : 2 * count], refs[2 * count : 3 * count]
     come, go = refs[3 * count :]
-    inward = [pltpu.make_async_copy(ins[i], held[i], come.at[i]) for i in range(count)]
-    outward = [pltpu.make_async_copy(held[i], outs[i], go.at[i]) for i in range(count)]
-    for copy in inward:
-        copy.start()
-    for i in range(count):
-        inward[i].wait()
-        outward[i].start()
-    for copy in outward:
-        copy.wait()
+    ways = []
+    for way in zip(ins, outs, held):
+        for source, target, stage in zip(*map(pieces_of_result, way)):
+            i = len(ways)
+            ways.append(
+                (
+                    pltpu.make_async_copy(source, stage, come.at[i]),
+                    pltpu.make_async_copy(stage, target, go.at[i]),
+                )
+            )
+    for inward, _ in ways:
+        inward.start()
+    for inward, outward in ways:
+        inward.wait()
+        outward.start()
+    for _, outward in ways:
+        outward.wait()
 
 
 def full(shape, dtype):
@@ -1214,7 +1241,7 @@
         in_specs=[hbm] * len(results),
         out_specs=(hbm,) * len(results),
         scratch_shapes=[VMEM(leaf.shape, leaf.dtype) for leaf in outs.values()]
-        + [dma((len(results),)), dma((len(results),))],
+        + [dma((32,)), dma((32,))],
     )(*results)
     found, grad_pieces, *others = results
     return (found, jnp.transpose(grad_pieces, (1, 0, 2)), *others)

time: 106 us -> 106 us (level)
  no operation moved by 1% of the time
where the time goes in v3:
time: 106 us
  Pallas kernels  105 us (99%)
    pallas_call x1, Pallas kernels, body(): pl.pallas_call(functools.partial(main_kernel, n_entries, tuple(ins) + tup...  102 us
    pallas_call x1, Pallas kernels, body(): pl.pallas_call(functools.partial(copy_kernel, len(results)), out_shape=tu...  3.09 us

profile of v3, /device:TPU:0, one launch (start us, length us, event | category | flops | bytes accessed | tf_op | source)
XLA Modules:
  0.0 105.6 jit_solution(2916685538405349979)
XLA Ops:
  0.6 101.7 %shard_map.213 = (bf16[64,9344]{1,0:T(8,128)(2,1)}, bf16[7,146,512]{2,1,0:T(8,128)(2,1)}, f32[4,16]{1,0:T(4,128)}, f32[16]{0:T(128)}, f32[16,1536]{1,0:T(8,128)}...) custom-call(bf16[7,146,512]{2,1,0:T(8,128)(2,1)} %bitcast.2, ...), custom_call_target="tpu_custom_call" | custom-call | tf_op jit(solution)/shard_map/pallas_call | solution.py:1221
  102.3 3.1 %shard_map.214 = (bf16[64,9344]{1,0:T(8,128)(2,1)}, bf16[7,146,512]{2,1,0:T(8,128)(2,1)}, f32[4,16]{1,0:T(4,128)}, f32[16]{0:T(128)}, f32[16,1536]{1,0:T(8,128)}...) custom-call(bf16[64,9344]{1,0:T(8,128)(2,1)} %get-tuple-element.30.refs_0_,, ...), custom_call_target="tpu_custom_call" | custom-call | tf_op jit(solution)/shard_map/pallas_call | solution.py:1238

commit v4 on v3

--- a/solution.py
+++ b/solution.py
@@ -851,6 +851,10 @@
 
     def result(part):
         stage = part.stage
+        if part is reduce.out:
+            for name in SUMS:
+                if name != "out":
+                    getattr(reduce, name).finish()
         part.z_wait(stage)
         if part is reduce.out:
             small = jnp.concatenate(
@@ -870,6 +874,7 @@
 
     def sent_all():
         exchange_wait(*grad_way, True)
+        exchange_wait(*table_way, True)
         for name in NAMES:
             getattr(gather, name).finish()
 
@@ -1064,9 +1069,7 @@
     result(reduce.v)
     result(reduce.q)
     result(reduce.out)
-    exchange_wait(*table_way, True)
-    for name in SUMS:
-        getattr(reduce, name).finish()
+    reduce.out.finish()
     for copy in going:
         copy.wait()
 

time: 106 us -> 106 us (level)
  no operation moved by 1% of the time
where the time goes in v4:
time: 106 us
  Pallas kernels  105 us (99%)
    pallas_call x1, Pallas kernels, body(): pl.pallas_call(functools.partial(main_kernel, n_entries, tuple(ins) + tup...  102 us
    pallas_call x1, Pallas kernels, body(): pl.pallas_call(functools.partial(copy_kernel, len(results)), out_shape=tu...  3.09 us

profile of v4, /device:TPU:0, one launch (start us, length us, event | category | flops | bytes accessed | tf_op | source)
XLA Modules:
  0.0 105.7 jit_solution(13961204001741465257)
XLA Ops:
  0.6 101.7 %shard_map.213 = (bf16[64,9344]{1,0:T(8,128)(2,1)}, bf16[7,146,512]{2,1,0:T(8,128)(2,1)}, f32[4,16]{1,0:T(4,128)}, f32[16]{0:T(128)}, f32[16,1536]{1,0:T(8,128)}...) custom-call(bf16[7,146,512]{2,1,0:T(8,128)(2,1)} %bitcast.2, ...), custom_call_target="tpu_custom_call" | custom-call | tf_op jit(solution)/shard_map/pallas_call | solution.py:1224
  102.4 3.1 %shard_map.214 = (bf16[64,9344]{1,0:T(8,128)(2,1)}, bf16[7,146,512]{2,1,0:T(8,128)(2,1)}, f32[4,16]{1,0:T(4,128)}, f32[16]{0:T(128)}, f32[16,1536]{1,0:T(8,128)}...) custom-call(bf16[64,9344]{1,0:T(8,128)(2,1)} %get-tuple-element.30.refs_0_,, ...), custom_call_target="tpu_custom_call" | custom-call | tf_op jit(solution)/shard_map/pallas_call | solution.py:1241
